TPU v7x, 32 devices: a whole 2x2x4 slice. The times are simulated.
32 devices in a mesh: shard: 4 (over z), ctx: 4 (over y, x), tp: 2 (over core).
Axes of the slice: x: 2, y: 2, z: 4, core: 2. Of those that a mesh axis runs over, the one named last changes fastest.
Arguments:
- tokens: bfloat16 [8, 1024, 768], P('shard', 'ctx'), may hold values from -6 to 6
- lengths: int32 [8], P('shard'), may hold values from 256 to 1024, as said below
- norm1_gain: bfloat16 [768], P('shard'), may hold values from 0.5 to 1.5
- qkv_weight: bfloat16 [768, 3, 768], P('shard', None, 'tp'), may hold values from -0.21875 to 0.21875
- lr_weight: bfloat16 [768, 12], P('shard', 'tp'), may hold values from -0.4375 to 0.4375
- inner_w1: bfloat16 [12, 64, 256], P('tp', None, 'shard'), may hold values from -0.75 to 0.75
- inner_b1: bfloat16 [12, 256], P('tp', 'shard'), may hold values from -4 to 4
- inner_w2: bfloat16 [12, 64, 256], P('tp', None, 'shard'), may hold values from -0.375 to 0.375
- inner_b2: bfloat16 [12, 64], P('tp', 'shard'), may hold values from -4 to 4
- post_gain: bfloat16 [12, 64], P('tp', 'shard'), may hold values from 0.5 to 1.5
- post_bias: bfloat16 [12, 64], P('tp', 'shard'), may hold values from -4 to 4
- gate_weight: bfloat16 [768, 768], P('shard', 'tp'), may hold values from -0.21875 to 0.21875
- out_weight: bfloat16 [768, 768], P('tp', 'shard'), may hold values from -0.21875 to 0.21875
- norm2_gain: bfloat16 [768], P('shard'), may hold values from 0.5 to 1.5
- ffn_gate: bfloat16 [768, 2048], P('shard', 'tp'), may hold values from -0.21875 to 0.21875
- ffn_up: bfloat16 [768, 2048], P('shard', 'tp'), may hold values from -0.21875 to 0.21875
- ffn_down: bfloat16 [2048, 768], P('tp', 'shard'), may hold values from -0.125 to 0.125
- cotangent: bfloat16 [8, 1024, 768], P('shard', 'ctx'), may hold values from -6 to 6
Outputs:
- output: bfloat16 [8, 1024, 768], P('shard', 'ctx')
- input_grad: bfloat16 [8, 1024, 768], P('shard', 'ctx')
- grad_norm1_gain: float32 [768], P('shard')
- grad_qkv_weight: float32 [768, 3, 768], P('shard', None, 'tp')
- grad_lr_weight: float32 [768, 12], P('shard', 'tp')
- grad_inner_w1: float32 [12, 64, 256], P('tp', None, 'shard')
- grad_inner_b1: float32 [12, 256], P('tp', 'shard')
- grad_inner_w2: float32 [12, 64, 256], P('tp', None, 'shard')
- grad_inner_b2: float32 [12, 64], P('tp', 'shard')
- grad_post_gain: float32 [12, 64], P('tp', 'shard')
- grad_post_bias: float32 [12, 64], P('tp', 'shard')
- grad_gate_weight: float32 [768, 768], P('shard', 'tp')
- grad_out_weight: float32 [768, 768], P('tp', 'shard')
- grad_norm2_gain: float32 [768], P('shard')
- grad_ffn_gate: float32 [768, 2048], P('shard', 'tp')
- grad_ffn_up: float32 [768, 2048], P('shard', 'tp')
- grad_ffn_down: float32 [2048, 768], P('tp', 'shard')
Inputs may be any that keep to these rules, and one draw needn't show every extreme that they name: Slot b holds lengths[b] valid positions at its start and padding after them; in every draw some slot is full.
All inputs are finite; a program needn't handle non-finite values.
Results may differ from a plain program's by a relative error of at most 0.0085.
Values may be sent and summed in bfloat16 or wider, within the bound.
No kernel may reach another device: no remote copies, remote signals or barrier semaphores. Data moves between devices by JAX's collectives and lax.ppermute only.
A program may use at most 192 MiB of HBM per device.

v0:
```python
from functools import partial

import jax
import jax.numpy as jnp
from jax import lax
from jax.sharding import PartitionSpec as P

MINI = 16


EPSILON = 1e-06
ETA_BASE = 0.5
HIGHEST = lax.Precision.HIGHEST


def passed_along(value, axis, steps):
    count = lax.axis_size(axis)
    leading, last = (max(0, -steps), min(count, count - steps))
    return lax.ppermute(value, axis, [(source, source + steps) for source in range(leading, last)])


def gelu(value):
    return jax.nn.gelu(value, approximate=False)


def gelu_slope(value):
    return (
        0.5 * (1.0 + lax.erf(value * 0.7071067811865476))
        + value * jnp.exp(-0.5 * value * value) * 0.3989422804014327
    )


def contract(form, left, right):
    return jnp.einsum(form, left, right, precision=HIGHEST)


def inner_step(state, block):
    first, first_bias, second, second_bias = state
    queries, keys, values, rates = block
    width = queries.shape[-2]
    row_index = lax.broadcasted_iota(jnp.int32, (width, width), 0)
    col_index = lax.broadcasted_iota(jnp.int32, (width, width), 1)
    scale = jnp.where(col_index <= row_index, 1.0 / (row_index + 1).astype(jnp.float32), 0.0)
    mix_rate = scale * rates[..., None, :]
    key_pre = contract("...bi,...ij->...bj", keys, first) + first_bias[..., None, :]
    key_act = gelu(key_pre)
    key_out = contract("...bj,...oj->...bo", key_act, second) + second_bias[..., None, :]
    grad_two = key_out + keys - values
    grad_one = contract("...bo,...oj->...bj", grad_two, second) * gelu_slope(key_pre)
    mix_one = mix_rate * (contract("...ti,...si->...ts", queries, keys) + 1.0)
    query_pre = (
        contract("...ti,...ij->...tj", queries, first)
        + first_bias[..., None, :]
        - contract("...ts,...sj->...tj", mix_one, grad_one)
    )
    query_act = gelu(query_pre)
    mix_two = mix_rate * (contract("...tj,...sj->...ts", query_act, key_act) + 1.0)
    query_out = (
        contract("...tj,...oj->...to", query_act, second)
        + second_bias[..., None, :]
        - contract("...ts,...so->...to", mix_two, grad_two)
    )
    result = queries + query_out
    final_rate = rates[..., :, None] / width
    step_one = final_rate * grad_one
    step_two = final_rate * grad_two
    first = first - contract("...bi,...bj->...ij", keys, step_one)
    first_bias = first_bias - jnp.sum(step_one, axis=-2)
    second = second - contract("...bo,...bj->...oj", step_two, key_act)
    second_bias = second_bias - jnp.sum(step_two, axis=-2)
    return ((first, first_bias, second, second_bias), result)


def rms_norm(value, gain):
    return value * lax.rsqrt(jnp.mean(value * value, axis=-1, keepdims=True) + EPSILON) * gain


def head_norm(value, gain, bias):
    centered = value - jnp.mean(value, axis=-1, keepdims=True)
    spread = jnp.mean(centered * centered, axis=-1, keepdims=True)
    return centered * lax.rsqrt(spread + EPSILON) * gain + bias


def pack_state(first, first_bias, second, second_bias):
    heads, width, inner = first.shape
    tail_row = jnp.zeros((heads, 1, inner), jnp.float32).at[:, 0, :width].set(second_bias)
    return jnp.concatenate([first, second, first_bias[:, None, :], tail_row], axis=1)


def unpack_state(packed, width):
    return (
        packed[:, :width],
        packed[:, 2 * width],
        packed[:, width : 2 * width],
        packed[:, 2 * width + 1, :width],
    )


def run_block(queries, keys, values, rates, live, packed):
    heads, width = (queries.shape[1], queries.shape[2])
    count = queries.shape[0] // MINI

    def to_blocks(value):
        return value.reshape(count, MINI, heads, width).transpose(0, 2, 1, 3)

    eta = ETA_BASE / width * jax.nn.sigmoid(rates) * live[:, None]
    rate_blocks = eta.reshape(count, MINI, heads).transpose(0, 2, 1)
    final, results = lax.scan(
        inner_step,
        unpack_state(packed, width),
        (to_blocks(queries), to_blocks(keys), to_blocks(values), rate_blocks),
    )
    return (results.transpose(0, 2, 1, 3).reshape(queries.shape), pack_state(*final))


def staggered_place(outer_turn, inner_turn, place, micro):
    which = inner_turn - place
    valid = jnp.logical_and(which >= 0, which < micro)
    return (jnp.clip(which, 0, micro - 1), valid)


def forward_chain(queries, keys, values, rates, live, init_packed, outer, inner, locate):
    place = lax.axis_index("ctx")
    micro = queries.shape[0]

    def forward_inner_body(turn, carry, outer_turn):
        received, outputs, kept = carry
        which, valid = locate(outer_turn, turn, place, micro)
        start = jnp.where(place == 0, init_packed, received)

        def forward_work():
            return run_block(
                queries[which], keys[which], values[which], rates[which], live[which], start
            )

        def forward_rest():
            return (jnp.zeros(queries.shape[1:], jnp.float32), start)

        result, leaving = lax.cond(valid, forward_work, forward_rest)
        outputs = outputs.at[which].set(jnp.where(valid, result, outputs[which]))
        kept = kept.at[which].set(jnp.where(valid, start, kept[which]))
        received = passed_along(leaving, "ctx", 1)
        return (received, outputs, kept)

    def forward_outer_body(outer_turn, carry):
        return lax.fori_loop(0, inner, partial(forward_inner_body, outer_turn=outer_turn), carry)

    start_carry = (
        jnp.zeros_like(init_packed),
        jnp.zeros(queries.shape, jnp.float32),
        jnp.zeros((micro,) + init_packed.shape, jnp.float32),
    )
    _, outputs, kept = lax.fori_loop(0, outer, forward_outer_body, start_carry)
    return (outputs, kept)


def backward_chain(queries, keys, values, rates, live, kept, grads_mixed, outer, inner, locate):
    first_device = lax.axis_index("ctx") == 0
    place = lax.axis_size("ctx") - 1 - lax.axis_index("ctx")
    micro = queries.shape[0]

    def backward_inner_body(turn, carry, outer_turn):
        received, grad_q, grad_k, grad_v, grad_r, total = carry
        which, valid = locate(outer_turn, turn, place, micro)

        def backward_work():

            def local(query_in, key_in, value_in, rate_in, packed):
                return run_block(query_in, key_in, value_in, rate_in, live[which], packed)

            _, pull = jax.vjp(
                local, queries[which], keys[which], values[which], rates[which], kept[which]
            )
            return pull((grads_mixed[which], received))

        def backward_rest():
            zeros = jnp.zeros(queries.shape[1:], jnp.float32)
            return (
                zeros,
                zeros,
                zeros,
                jnp.zeros(rates.shape[1:], jnp.float32),
                jnp.zeros_like(received),
            )

        part_q, part_k, part_v, part_r, part_state = lax.cond(valid, backward_work, backward_rest)
        grad_q = grad_q.at[which].set(jnp.where(valid, part_q, grad_q[which]))
        grad_k = grad_k.at[which].set(jnp.where(valid, part_k, grad_k[which]))
        grad_v = grad_v.at[which].set(jnp.where(valid, part_v, grad_v[which]))
        grad_r = grad_r.at[which].set(jnp.where(valid, part_r, grad_r[which]))
        total = total + jnp.where(jnp.logical_and(valid, first_device), part_state, 0.0)
        received = passed_along(part_state, "ctx", -1)
        return (received, grad_q, grad_k, grad_v, grad_r, total)

    def backward_outer_body(outer_turn, carry):
        return lax.fori_loop(0, inner, partial(backward_inner_body, outer_turn=outer_turn), carry)

    zeros = jnp.zeros(queries.shape, jnp.float32)
    start_carry = (
        jnp.zeros(kept.shape[1:], jnp.float32),
        zeros,
        zeros,
        zeros,
        jnp.zeros(rates.shape, jnp.float32),
        jnp.zeros(kept.shape[1:], jnp.float32),
    )
    _, grad_q, grad_k, grad_v, grad_r, total = lax.fori_loop(
        0, outer, backward_outer_body, start_carry
    )
    return (grad_q, grad_k, grad_v, grad_r, total)


def on_device(
    tokens,
    lengths,
    norm1_gain,
    qkv_weight,
    lr_weight,
    inner_w1,
    inner_b1,
    inner_w2,
    inner_b2,
    post_gain,
    post_bias,
    gate_weight,
    out_weight,
    norm2_gain,
    ffn_gate,
    ffn_up,
    ffn_down,
    cotangent,
):
    full = (
        lax.all_gather(norm1_gain, "shard", axis=0, tiled=True),
        lax.all_gather(qkv_weight, "shard", axis=0, tiled=True),
        lax.all_gather(lr_weight, "shard", axis=0, tiled=True),
        lax.all_gather(inner_w1, "shard", axis=2, tiled=True),
        lax.all_gather(inner_b1, "shard", axis=1, tiled=True),
        lax.all_gather(inner_w2, "shard", axis=2, tiled=True),
        lax.all_gather(inner_b2, "shard", axis=1, tiled=True),
        lax.all_gather(post_gain, "shard", axis=1, tiled=True),
        lax.all_gather(post_bias, "shard", axis=1, tiled=True),
        lax.all_gather(gate_weight, "shard", axis=0, tiled=True),
        lax.all_gather(out_weight, "shard", axis=1, tiled=True),
        lax.all_gather(norm2_gain, "shard", axis=0, tiled=True),
        lax.all_gather(ffn_gate, "shard", axis=0, tiled=True),
        lax.all_gather(ffn_up, "shard", axis=0, tiled=True),
        lax.all_gather(ffn_down, "shard", axis=1, tiled=True),
    )
    (
        gain_one,
        w_qkv,
        w_rate,
        init_first,
        init_first_bias,
        init_second,
        init_second_bias,
        norm_gain,
        norm_bias,
        w_gate,
        w_out,
        gain_two,
        w_ffn_gate,
        w_ffn_up,
        w_ffn_down,
    ) = full
    micro, span, width = tokens.shape
    rows = micro * span
    heads = w_rate.shape[1]
    head_dim = init_first.shape[1]
    position = lax.axis_index("ctx") * span + lax.broadcasted_iota(jnp.int32, (micro, span), 1)
    live = (position < lengths[:, None]).astype(jnp.float32)
    inputs = tokens.astype(jnp.float32).reshape(rows, width)
    gain_one_f = gain_one.astype(jnp.float32)
    gain_two_f = gain_two.astype(jnp.float32)
    normed_one = rms_norm(inputs, gain_one_f).astype(jnp.bfloat16)
    flat_qkv = w_qkv.reshape(width, -1)
    projected = jnp.dot(normed_one, flat_qkv, preferred_element_type=jnp.float32).reshape(
        micro, span, 3, heads, head_dim
    )
    rates = jnp.dot(normed_one, w_rate, preferred_element_type=jnp.float32).reshape(
        micro, span, heads
    )
    gate_pre = jnp.dot(normed_one, w_gate, preferred_element_type=jnp.float32)
    init_packed = pack_state(
        init_first.astype(jnp.float32),
        init_first_bias.astype(jnp.float32),
        init_second.astype(jnp.float32),
        init_second_bias.astype(jnp.float32),
    )
    outer, inner, locate = (1, lax.axis_size("ctx") + micro - 1, staggered_place)
    queries = projected[:, :, 0]
    keys = projected[:, :, 1]
    values = projected[:, :, 2]
    mixed, kept = forward_chain(
        queries, keys, values, rates, live, init_packed, outer, inner, locate
    )

    def post_fn(gate_in, mixed_in, gain_in, bias_in):
        return gelu(gate_in) * head_norm(mixed_in, gain_in, bias_in).reshape(rows, -1)

    post, post_pull = jax.vjp(
        post_fn,
        gate_pre,
        mixed.reshape(rows, heads, head_dim),
        norm_gain.astype(jnp.float32),
        norm_bias.astype(jnp.float32),
    )
    post_low = post.astype(jnp.bfloat16)
    branch = lax.psum(jnp.dot(post_low, w_out, preferred_element_type=jnp.float32), "tp")
    hidden = inputs + branch
    normed_two, norm_two_pull = jax.vjp(rms_norm, hidden, gain_two_f)
    normed_two_low = normed_two.astype(jnp.bfloat16)
    up_gate = jnp.dot(normed_two_low, w_ffn_gate, preferred_element_type=jnp.float32)
    up_lin = jnp.dot(normed_two_low, w_ffn_up, preferred_element_type=jnp.float32)
    act, act_pull = jax.vjp(lambda left, right: jax.nn.silu(left) * right, up_gate, up_lin)
    act_low = act.astype(jnp.bfloat16)
    feed = lax.psum(jnp.dot(act_low, w_ffn_down, preferred_element_type=jnp.float32), "tp")
    output = (hidden + feed).reshape(micro, span, width).astype(jnp.bfloat16)
    back = cotangent.astype(jnp.float32).reshape(rows, width) * live.reshape(rows, 1)
    back_low = back.astype(jnp.bfloat16)
    g_ffn_down = jnp.einsum("rf,rd->fd", act_low, back_low, preferred_element_type=jnp.float32)
    grad_act = jnp.einsum("rd,fd->rf", back_low, w_ffn_down, preferred_element_type=jnp.float32)
    grad_gate_ffn, grad_lin_ffn = act_pull(grad_act)
    grad_gate_low = grad_gate_ffn.astype(jnp.bfloat16)
    grad_lin_low = grad_lin_ffn.astype(jnp.bfloat16)
    g_ffn_gate = jnp.einsum(
        "rd,rf->df", normed_two_low, grad_gate_low, preferred_element_type=jnp.float32
    )
    g_ffn_up = jnp.einsum(
        "rd,rf->df", normed_two_low, grad_lin_low, preferred_element_type=jnp.float32
    )
    back_two = jnp.einsum(
        "rf,df->rd", grad_gate_low, w_ffn_gate, preferred_element_type=jnp.float32
    ) + jnp.einsum("rf,df->rd", grad_lin_low, w_ffn_up, preferred_element_type=jnp.float32)
    back_two = lax.psum(back_two, "tp")
    grad_hidden_part, g_gain_two = norm_two_pull(back_two)
    grad_hidden = back + grad_hidden_part
    grad_hidden_low = grad_hidden.astype(jnp.bfloat16)
    g_out = jnp.einsum("rh,rd->hd", post_low, grad_hidden_low, preferred_element_type=jnp.float32)
    grad_post = jnp.einsum("rd,hd->rh", grad_hidden_low, w_out, preferred_element_type=jnp.float32)
    grad_gate_in, grad_mixed, g_norm_gain, g_norm_bias = post_pull(grad_post)
    grad_q, grad_k, grad_v, grad_r, total = backward_chain(
        queries,
        keys,
        values,
        rates,
        live,
        kept,
        grad_mixed.reshape(micro, span, heads, head_dim),
        outer,
        inner,
        locate,
    )
    g_init_first, g_init_first_bias, g_init_second, g_init_second_bias = unpack_state(
        total, head_dim
    )
    grad_proj_low = (
        jnp.stack([grad_q, grad_k, grad_v], axis=2).reshape(rows, -1).astype(jnp.bfloat16)
    )
    grad_rate_low = grad_r.reshape(rows, heads).astype(jnp.bfloat16)
    grad_gate_pre_low = grad_gate_in.astype(jnp.bfloat16)
    g_qkv = jnp.einsum(
        "rd,rc->dc", normed_one, grad_proj_low, preferred_element_type=jnp.float32
    ).reshape(w_qkv.shape)
    g_rate = jnp.einsum("rd,rh->dh", normed_one, grad_rate_low, preferred_element_type=jnp.float32)
    g_gate = jnp.einsum(
        "rd,rh->dh", normed_one, grad_gate_pre_low, preferred_element_type=jnp.float32
    )
    back_one = (
        jnp.einsum("rc,dc->rd", grad_proj_low, flat_qkv, preferred_element_type=jnp.float32)
        + jnp.einsum("rh,dh->rd", grad_rate_low, w_rate, preferred_element_type=jnp.float32)
        + jnp.einsum("rh,dh->rd", grad_gate_pre_low, w_gate, preferred_element_type=jnp.float32)
    )
    back_one = lax.psum(back_one, "tp")
    _, norm_one_pull = jax.vjp(rms_norm, inputs, gain_one_f)
    grad_in_part, g_gain_one = norm_one_pull(back_one)
    input_grad = (grad_hidden + grad_in_part).reshape(micro, span, width).astype(jnp.bfloat16)
    shares = (
        lax.psum_scatter(g_gain_one, "shard", scatter_dimension=0, tiled=True),
        lax.psum_scatter(g_qkv, "shard", scatter_dimension=0, tiled=True),
        lax.psum_scatter(g_rate, "shard", scatter_dimension=0, tiled=True),
        lax.psum_scatter(g_init_first, "shard", scatter_dimension=2, tiled=True),
        lax.psum_scatter(g_init_first_bias, "shard", scatter_dimension=1, tiled=True),
        lax.psum_scatter(g_init_second, "shard", scatter_dimension=2, tiled=True),
        lax.psum_scatter(g_init_second_bias, "shard", scatter_dimension=1, tiled=True),
        lax.psum_scatter(g_norm_gain, "shard", scatter_dimension=1, tiled=True),
        lax.psum_scatter(g_norm_bias, "shard", scatter_dimension=1, tiled=True),
        lax.psum_scatter(g_gate, "shard", scatter_dimension=0, tiled=True),
        lax.psum_scatter(g_out, "shard", scatter_dimension=1, tiled=True),
        lax.psum_scatter(g_gain_two, "shard", scatter_dimension=0, tiled=True),
        lax.psum_scatter(g_ffn_gate, "shard", scatter_dimension=0, tiled=True),
        lax.psum_scatter(g_ffn_up, "shard", scatter_dimension=0, tiled=True),
        lax.psum_scatter(g_ffn_down, "shard", scatter_dimension=1, tiled=True),
    )
    shares = lax.psum(
        (
            shares[0],
            shares[1],
            shares[2],
            shares[3],
            shares[4],
            shares[5],
            shares[6],
            shares[7],
            shares[8],
            shares[9],
            shares[10],
            shares[11],
            shares[12],
            shares[13],
            shares[14],
        ),
        "ctx",
    )
    return (
        output,
        input_grad,
        shares[0],
        shares[1],
        shares[2],
        shares[3],
        shares[4],
        shares[5],
        shares[6],
        shares[7],
        shares[8],
        shares[9],
        shares[10],
        shares[11],
        shares[12],
        shares[13],
        shares[14],
    )


def solution(mesh):
    in_specs = (
        P("shard", "ctx", None),
        P("shard"),
        P("shard"),
        P("shard", None, "tp"),
        P("shard", "tp"),
        P("tp", None, "shard"),
        P("tp", "shard"),
        P("tp", None, "shard"),
        P("tp", "shard"),
        P("tp", "shard"),
        P("tp", "shard"),
        P("shard", "tp"),
        P("tp", "shard"),
        P("shard"),
        P("shard", "tp"),
        P("shard", "tp"),
        P("tp", "shard"),
        P("shard", "ctx", None),
    )
    out_specs = (
        P("shard", "ctx", None),
        P("shard", "ctx", None),
        P("shard"),
        P("shard", None, "tp"),
        P("shard", "tp"),
        P("tp", None, "shard"),
        P("tp", "shard"),
        P("tp", None, "shard"),
        P("tp", "shard"),
        P("tp", "shard"),
        P("tp", "shard"),
        P("shard", "tp"),
        P("tp", "shard"),
        P("shard"),
        P("shard", "tp"),
        P("shard", "tp"),
        P("tp", "shard"),
    )
    return jax.shard_map(
        on_device, mesh=mesh, in_specs=in_specs, out_specs=out_specs, check_vma=False
    )
```

profile of v0, /device:TPU:12, one launch (start us, length us, event | category | flops | bytes accessed | tf_op | source)
XLA Modules:
  0.0 5403.7 jit_solution(8606063000714283316)
XLA Ops:
  171.6 968.6 %while.196 = (s32[]{:T(128)}, f32[6,130,256]{2,1,0:T(8,128)}, f32[2,256,6,64]{3,2,1,0:T(8,128)S(1)}, f32[2,6,130,256]{3,2,1,0:T(8,128)}, s32[]{:T(128)}, /*index...) while((s32[]{:T(128)}, f32[6,130,256]{2,1,0:T(8,128)}, ...), condition=%wide.region_9.10_spmd.clone, body=%wide.region_1.9_spmd.clone.sunk | while | flops 150363056 | bytes 44140444 | solution.py:146
  208.4 349.5 %collective-permute-done.1 = f32[6,130,256]{2,1,0:T(8,128)} collective-permute-done((f32[6,130,256]{2,1,0:T(8,128)}, f32[6,130,256]{2,1,0:T(8,128)}, u32[]{:S(2)}, u32[]{:S(2)}) %collective-permute-start.1) | collective-permute-done | bytes 798752 | tf_op jit(solution)/shard_map/while/body/eval_jaxpr/while/body/eval_jaxpr/ppermute | solution.py:19
  564.2 173.6 %conditional.6 = (f32[256,6,64]{2,1,0:T(8,128)S(1)}, f32[6,130,256]{2,1,0:T(8,128)}) conditional(s32[]{:T(128)} %convert_element_type.219, f32[6,130,256]{2,1,0:T(8,128)} %get-tuple-element.3851, (f32[6,130,256]{2,1,0:T(8,128)}, s32[]{:T(128)}, f32[2,256,6,64]{3,1,2,0:T(8,128)}, f32[2,256,6,64]{3,1,2,0:T(8,128)}, f32[2,256,6,64]{3,1,2,0:T(8,128)}, ...), branch_computations={%region_2.2_spmd, %region_3.7_spmd} | conditional | flops 149566352 | bytes 15419827 | solution.py:139
  571.7 164.3 %while.193 = (s32[]{:T(128)}, f32[6,64,256]{2,1,0:T(8,128)S(1)}, f32[6,256]{1,0:T(8,128)S(1)}, f32[6,64,256]{2,1,0:T(8,128)S(1)}, f32[6,64]{1,0:T(8,128)S(1)}, /...) while((s32[]{:T(128)}, f32[6,64,256]{2,1,0:T(8,128)S(1)}, ...), condition=%wide.region_7.6_spmd, body=%wide.region_4.0_spmd.sunk | while | flops 148561552 | bytes 5865205 | solution.py:108
  759.6 173.6 %conditional.6 = (f32[256,6,64]{2,1,0:T(8,128)S(1)}, f32[6,130,256]{2,1,0:T(8,128)}) conditional(s32[]{:T(128)} %convert_element_type.219, f32[6,130,256]{2,1,0:T(8,128)} %get-tuple-element.3851, (f32[6,130,256]{2,1,0:T(8,128)}, s32[]{:T(128)}, f32[2,256,6,64]{3,1,2,0:T(8,128)}, f32[2,256,6,64]{3,1,2,0:T(8,128)}, f32[2,256,6,64]{3,1,2,0:T(8,128)}, ...), branch_computations={%region_2.2_spmd, %region_3.7_spmd} | conditional | flops 149566352 | bytes 15419827 | solution.py:139
  767.2 164.3 %while.193 = (s32[]{:T(128)}, f32[6,64,256]{2,1,0:T(8,128)S(1)}, f32[6,256]{1,0:T(8,128)S(1)}, f32[6,64,256]{2,1,0:T(8,128)S(1)}, f32[6,64]{1,0:T(8,128)S(1)}, /...) while((s32[]{:T(128)}, f32[6,64,256]{2,1,0:T(8,128)S(1)}, ...), condition=%wide.region_7.6_spmd, body=%wide.region_4.0_spmd.sunk | while | flops 148561552 | bytes 5865205 | solution.py:108
  957.2 172.4 %collective-permute-start.1 = (f32[6,130,256]{2,1,0:T(8,128)}, f32[6,130,256]{2,1,0:T(8,128)}, u32[]{:S(2)}, u32[]{:S(2)}) collective-permute-start(f32[6,130,256]{2,1,0:T(8,128)} %get-tuple-element.3852), channel_id=1, source_target_pairs={{0,2},{2,4},{4,6},{1,3},{3,5},{5,7},{8,10},{10,12},{12,14},{9,11},... | collective-permute-start | bytes 2396168 | tf_op jit(solution)/shard_map/while/body/eval_jaxpr/while/body/eval_jaxpr/ppermute | solution.py:19
  1178.9 35.6 all-gather.12.cloned.1.call-done
  1255.7 33.8 all-gather.16.cloned.1.call-done
  1341.4 2786.1 %while.197 = (s32[]{:T(128)}, f32[6,130,256]{2,1,0:T(8,128)}, bf16[2,256,6,64]{1,3,2,0:T(8,128)(2,1)}, bf16[2,256,6,64]{1,3,2,0:T(8,128)(2,1)}, bf16[2,256,6,64]...) while((s32[]{:T(128)}, f32[6,130,256]{2,1,0:T(8,128)}, ...), condition=%wide.region_37.38_spmd.clone, body=%wide.region_19.37_spmd.clone.sunk | while | flops 422240704 | bytes 80312808 | solution.py:196
  1373.7 665.0 %collective-permute-done = f32[6,130,256]{2,1,0:T(8,128)S(1)} collective-permute-done((f32[6,130,256]{2,1,0:T(8,128)}, f32[6,130,256]{2,1,0:T(8,128)S(1)}, u32[]{:S(2)}, u32[]{:S(2)}) %collective-permute-start) | collective-permute-done | bytes 798752 | tf_op jit(solution)/shard_map/while/body/eval_jaxpr/while/body/eval_jaxpr/ppermute | solution.py:19
  2040.2 662.9 %conditional.7 = (bf16[256,6,64]{2,1,0:T(8,128)(2,1)}, bf16[256,6,64]{2,1,0:T(8,128)(2,1)}, bf16[256,6,64]{2,1,0:T(8,128)(2,1)}, bf16[256,6]{0,1:T(8,128)(2,1)S(1)}, f32[6,130,256]{2,0,1:T(8,128)S(1)}) conditional(s32[]{:T(128)} %convert_element_type.221, () %tuple.342, (f32[6,130,256]{2,1,0:T(8,128)}, s32[]{:T(128)}, ...), branch_computations={%region_20.20_spmd, %region_21.34_spmd} | conditional | flops 421047680 | bytes 53096116 | solution.py:186
  2048.6 181.2 %while.195 = (s32[]{:T(128)}, f32[6,64,256]{2,1,0:T(8,128)S(1)}, f32[6,256]{1,0:T(8,128)S(1)}, f32[6,64,256]{2,1,0:T(8,128)S(1)}, f32[6,64]{1,0:T(8,128)S(1)}, /...) while((s32[]{:T(128)}, f32[6,64,256]{2,1,0:T(8,128)S(1)}, ...), condition=%wide.region_25.24_spmd.clone.clone, body=%wide.region_22.23_spmd.clone.clone.sunk | while | flops 130390720 | bytes 8892701 | solution.py:108
  2232.5 467.1 %while.194 = (s32[]{:T(128)}, f32[6,64,256]{2,1,0:T(8,128)S(1)}, f32[6,256]{1,0:T(8,128)S(1)}, f32[6,64,256]{2,1,0:T(8,128)S(1)}, f32[6,64]{1,0:T(8,128)S(1)}, /...) while((s32[]{:T(128)}, f32[6,64,256]{2,1,0:T(8,128)S(1)}, ...), condition=%wide.region_34.33_spmd.clone, body=%wide.region_26.32_spmd.clone.sunk | while | flops 289939328 | bytes 13489109 | solution.py:108
  2728.2 662.9 %conditional.7 = (bf16[256,6,64]{2,1,0:T(8,128)(2,1)}, bf16[256,6,64]{2,1,0:T(8,128)(2,1)}, bf16[256,6,64]{2,1,0:T(8,128)(2,1)}, bf16[256,6]{0,1:T(8,128)(2,1)S(1)}, f32[6,130,256]{2,0,1:T(8,128)S(1)}) conditional(s32[]{:T(128)} %convert_element_type.221, () %tuple.342, (f32[6,130,256]{2,1,0:T(8,128)}, s32[]{:T(128)}, ...), branch_computations={%region_20.20_spmd, %region_21.34_spmd} | conditional | flops 421047680 | bytes 53096116 | solution.py:186
  2736.6 181.2 %while.195 = (s32[]{:T(128)}, f32[6,64,256]{2,1,0:T(8,128)S(1)}, f32[6,256]{1,0:T(8,128)S(1)}, f32[6,64,256]{2,1,0:T(8,128)S(1)}, f32[6,64]{1,0:T(8,128)S(1)}, /...) while((s32[]{:T(128)}, f32[6,64,256]{2,1,0:T(8,128)S(1)}, ...), condition=%wide.region_25.24_spmd.clone.clone, body=%wide.region_22.23_spmd.clone.clone.sunk | while | flops 130390720 | bytes 8892701 | solution.py:108
  2920.5 467.1 %while.194 = (s32[]{:T(128)}, f32[6,64,256]{2,1,0:T(8,128)S(1)}, f32[6,256]{1,0:T(8,128)S(1)}, f32[6,64,256]{2,1,0:T(8,128)S(1)}, f32[6,64]{1,0:T(8,128)S(1)}, /...) while((s32[]{:T(128)}, f32[6,64,256]{2,1,0:T(8,128)S(1)}, ...), condition=%wide.region_34.33_spmd.clone, body=%wide.region_26.32_spmd.clone.sunk | while | flops 289939328 | bytes 13489109 | solution.py:108
  3419.0 664.7 %collective-permute-start = (f32[6,130,256]{2,1,0:T(8,128)}, f32[6,130,256]{2,1,0:T(8,128)S(1)}, u32[]{:S(2)}, u32[]{:S(2)}) collective-permute-start(f32[6,130,256]{2,1,0:T(8,128)} %copy.443), channel_id=1, source_target_pairs={{2,0},{4,2},{6,4},{3,1},{5,3},{7,5},{10,8},{12,10},{14,12},{11,9},... | collective-permute-start | bytes 2396168 | tf_op jit(solution)/shard_map/while/body/eval_jaxpr/while/body/eval_jaxpr/ppermute | solution.py:19
  4174.9 632.8 %reduce-scatter.42.cloned.1.call-done = f32[64,384]{1,0:T(8,128)} async-done(((f32[256,384]{1,0:T(8,128)}), f32[64,384]{1,0:T(8,128)}) %reduce-scatter.42.cloned.1.call-update) | async-done | bytes 98320
  4890.6 62.8 %reduce-scatter.34.cloned.1.call-done = f32[192,1024]{1,0:T(8,128)} async-done(((f32[768,1024]{1,0:T(8,128)}), f32[192,1024]{1,0:T(8,128)}) %reduce-scatter.34.cloned.1.call-update) | async-done | bytes 786448 | tf_op jit(solution)/shard_map/reduce_scatter | solution.py:392
  4953.4 62.5 %reduce-scatter.36.cloned.1.call-done = f32[192,1024]{1,0:T(8,128)} async-done(((f32[768,1024]{1,0:T(8,128)}), f32[192,1024]{1,0:T(8,128)}) %reduce-scatter.36.cloned.1.call-update) | async-done | bytes 786448 | tf_op jit(solution)/shard_map/reduce_scatter | solution.py:393
  5015.8 62.6 %reduce-scatter.38.cloned.1.call-done = f32[1024,192]{0,1:T(8,128)} async-done(((f32[1024,768]{0,1:T(8,128)}), f32[1024,192]{0,1:T(8,128)}) %reduce-scatter.38.cloned.1.call-update) | async-done | bytes 786448 | tf_op jit(solution)/shard_map/reduce_scatter | solution.py:394
  5078.5 68.9 %reduce-scatter.28.cloned.1.call-done = f32[192,3,384]{2,0,1:T(8,128)} async-done(((f32[768,3,384]{2,0,1:T(8,128)}), f32[192,3,384]{2,0,1:T(8,128)}) %reduce-scatter.28.cloned.1.call-update) | async-done | bytes 884752 | tf_op jit(solution)/shard_map/reduce_scatter | solution.py:381
  5307.2 81.5 %all-reduce.24.cloned.1.call-done = (f32[192,3,384]{2,0,1:T(8,128)}, f32[6,64,64]{2,1,0:T(8,128)}, f32[6,64,64]{2,1,0:T(8,128)}, f32[192,384]{1,0:T(8,128)}, f32...) async-done(((f32[192,3,384]{2,0,1:T(8,128)}, f32[6,64,64]{2,1,0:T(8,128)}, f32[6,64,64]{2,1,0:T(8,128)}, ...) | async-done | bytes 4030480 | tf_op jit(solution)/shard_map/psum | solution.py:396
  (3142 shorter events, 2476.3 us)
Async XLA Ops:
  7.2 150.4 %all-gather.10.cloned.1.call-start = ((), (), s32[]{:S(2)}) async-start(), calls=%async_computation.13 | async-start | bytes 2211840 | tf_op jit(solution)/shard_map/all_gather | solution.py:235
  7.9 1167.9 %all-reduce.20.cloned.1.call-start = ((), (), s32[]{:S(2)}) async-start(), calls=%async_computation.14 | async-start | bytes 3145728 | tf_op jit(solution)/shard_map/psum | solution.py:310
  202.0 356.0 %collective-permute-start.1 = (f32[6,130,256]{2,1,0:T(8,128)}, f32[6,130,256]{2,1,0:T(8,128)}, u32[]{:S(2)}, u32[]{:S(2)}) collective-permute-start(f32[6,130,256]{2,1,0:T(8,128)} %get-tuple-element.3852), channel_id=1, source_target_pairs={{0,2},{2,4},{4,6},{1,3},{3,5},{5,7},{8,10},{10,12},{12,14},{9,11},... | collective-permute-start | bytes 2396168 | tf_op jit(solution)/shard_map/while/body/eval_jaxpr/while/body/eval_jaxpr/ppermute | solution.py:19
  957.2 182.7 %collective-permute-start.1 = (f32[6,130,256]{2,1,0:T(8,128)}, f32[6,130,256]{2,1,0:T(8,128)}, u32[]{:S(2)}, u32[]{:S(2)}) collective-permute-start(f32[6,130,256]{2,1,0:T(8,128)} %get-tuple-element.3852), channel_id=1, source_target_pairs={{0,2},{2,4},{4,6},{1,3},{3,5},{5,7},{8,10},{10,12},{12,14},{9,11},... | collective-permute-start | bytes 2396168 | tf_op jit(solution)/shard_map/while/body/eval_jaxpr/while/body/eval_jaxpr/ppermute | solution.py:19
  1153.7 98.3 %all-gather.14.cloned.1.call-start = ((), (), s32[]{:S(2)}) async-start(), calls=%async_computation.16 | async-start | bytes 1966080 | tf_op jit(solution)/shard_map/all_gather | solution.py:247
  1154.3 135.2 %all-gather.16.cloned.1.call-start = ((), (), s32[]{:S(2)}) async-start(), calls=%async_computation.17 | async-start | bytes 1966080 | tf_op jit(solution)/shard_map/all_gather | solution.py:248
  1154.9 165.5 %all-reduce.22.cloned.1.call-start = ((), (), s32[]{:S(2)}) async-start(), calls=%async_computation.18 | async-start | bytes 3145728 | tf_op jit(solution)/shard_map/psum | solution.py:336
  1299.6 3508.1 %reduce-scatter.42.cloned.1.call-start = ((), (), s32[]{:S(2)}) async-start(), calls=%async_computation.26 | async-start | bytes 491520
  1356.4 682.4 %collective-permute-start = (f32[6,130,256]{2,1,0:T(8,128)}, f32[6,130,256]{2,1,0:T(8,128)S(1)}, u32[]{:S(2)}, u32[]{:S(2)}) collective-permute-start(f32[6,130,256]{2,1,0:T(8,128)} %copy.443), channel_id=1, source_target_pairs={{2,0},{4,2},{6,4},{3,1},{5,3},{7,5},{10,8},{12,10},{14,12},{11,9},... | collective-permute-start | bytes 2396168 | tf_op jit(solution)/shard_map/while/body/eval_jaxpr/while/body/eval_jaxpr/ppermute | solution.py:19
  3419.0 681.3 %collective-permute-start = (f32[6,130,256]{2,1,0:T(8,128)}, f32[6,130,256]{2,1,0:T(8,128)S(1)}, u32[]{:S(2)}, u32[]{:S(2)}) collective-permute-start(f32[6,130,256]{2,1,0:T(8,128)} %copy.443), channel_id=1, source_target_pairs={{2,0},{4,2},{6,4},{3,1},{5,3},{7,5},{10,8},{12,10},{14,12},{11,9},... | collective-permute-start | bytes 2396168 | tf_op jit(solution)/shard_map/while/body/eval_jaxpr/while/body/eval_jaxpr/ppermute | solution.py:19
  4130.5 699.1 %reduce-scatter.46.cloned.1.call-start = ((), (), s32[]{:S(2)}) async-start(), calls=%async_computation.28 | async-start | bytes 491520
  4132.0 728.4 %reduce-scatter.32.cloned.1.call-start = ((), (), s32[]{:S(2)}) async-start(), calls=%async_computation.21 | async-start | bytes 1474560 | tf_op jit(solution)/shard_map/reduce_scatter | solution.py:390
  4134.8 755.8 %reduce-scatter.30.cloned.1.call-start = ((), (), s32[]{:S(2)}) async-start(), calls=%async_computation.20 | async-start | bytes 1474560 | tf_op jit(solution)/shard_map/reduce_scatter | solution.py:389
  4137.7 815.7 %reduce-scatter.34.cloned.1.call-start = ((), (), s32[]{:S(2)}) async-start(), calls=%async_computation.22 | async-start | bytes 3932160 | tf_op jit(solution)/shard_map/reduce_scatter | solution.py:392
  4140.5 875.4 %reduce-scatter.36.cloned.1.call-start = ((), (), s32[]{:S(2)}) async-start(), calls=%async_computation.23 | async-start | bytes 3932160 | tf_op jit(solution)/shard_map/reduce_scatter | solution.py:393
  4144.4 934.0 %reduce-scatter.38.cloned.1.call-start = ((), (), s32[]{:S(2)}) async-start(), calls=%async_computation.24 | async-start | bytes 3932160 | tf_op jit(solution)/shard_map/reduce_scatter | solution.py:394
  4148.7 998.7 %reduce-scatter.28.cloned.1.call-start = ((), (), s32[]{:S(2)}) async-start(), calls=%async_computation.19 | async-start | bytes 4423680 | tf_op jit(solution)/shard_map/reduce_scatter | solution.py:381
  4155.4 1011.3 %reduce-scatter.48.cloned.1.call-start = ((), (), s32[]{:S(2)}) async-start(), calls=%async_computation.29 | async-start | bytes 40960
  4161.1 1025.4 %reduce-scatter.50.cloned.1.call-start = ((), (), s32[]{:S(2)}) async-start(), calls=%async_computation.30 | async-start | bytes 40960
  4165.9 1040.4 %reduce-scatter.52.cloned.1.call-start = ((), (), s32[]{:S(2)}) async-start(), calls=%async_computation.31 | async-start | bytes 40960
  4168.4 1058.0 %reduce-scatter.44.cloned.1.call-start = ((), (), s32[]{:S(2)}) async-start(), calls=%async_computation.27 | async-start | bytes 163840
  4170.0 1077.8 %reduce-scatter.40.cloned.1.call-start = ((), (), s32[]{:S(2)}) async-start(), calls=%async_computation.25 | async-start | bytes 491520
  4171.2 1103.8 %all-reduce.26.cloned.1.call-start = ((), (), s32[]{:S(2)}) async-start(), calls=%async_computation.33 | async-start | bytes 6291456 | tf_op jit(solution)/shard_map/psum | solution.py:318
  4174.6 1214.1 %all-reduce.24.cloned.1.call-start = ((), (), s32[]{:S(2)}) async-start(), calls=%async_computation.32 | async-start | bytes 8454144 | tf_op jit(solution)/shard_map/psum | solution.py:396
  (144 other events, 4144.5 us)
Sparse Core Ops, SparseCore 0:
  9.6 48.8 all-gather.9
  1153.1 22.7 all-reduce.19
  1177.5 36.9 all-gather.11
  1216.0 35.9 all-gather.13
  1253.5 35.9 all-gather.15
  1299.8 20.5 all-reduce.21
  4130.6 677.0 reduce-scatter.41
  4810.7 18.8 reduce-scatter.45
  4831.9 28.4 reduce-scatter.31
  4862.6 27.9 reduce-scatter.29
  4892.9 60.4 reduce-scatter.33
  4955.5 60.2 reduce-scatter.35
  5018.1 60.2 reduce-scatter.37
  5080.6 66.6 reduce-scatter.27
  5150.0 16.6 reduce-scatter.47
  5169.4 17.0 reduce-scatter.49
  5189.2 17.0 reduce-scatter.51
  5209.1 17.2 reduce-scatter.43
  5229.3 18.4 reduce-scatter.39
  5250.1 24.7 all-reduce.25
  5280.1 108.6 all-reduce.23
where the time goes:
time: 5460 us; the launch traced here: 5400 us
  waiting for transfers between devices  2380 us (44%)
  matrix products  1440 us (26%)
  starting transfers between devices  863 us (16%)
  local copies, waits for them, and re-layouts  298 us (5%)
  other arithmetic  211 us (4%)
  blocking collectives  165 us (3%)
    dot_general x1344, matrix products, contract(): return jnp.einsum(form, left, right, precision=HIGHEST)  1380 us
    ppermute x10, waiting for transfers between devices, passed_along(): lax.ppermute(value, axis, [(source, source + steps) for source in range(l...  1070 us
    ppermute x10, starting transfers between devices, passed_along(): lax.ppermute(value, axis, [(source, source + steps) for source in range(l...  862 us
    unnamed x28, waiting for transfers between devices  752 us
  transfers between devices with their start and end apart: 31, of which 30 were waited for; matrix products, arithmetic and copies ran while one was open for 3% of the time, Pallas kernels for 0%

commit v1 on v0

v1 whole, which is shorter than its diff:
```python
from functools import partial
import jax
import jax.numpy as jnp
from jax import lax
from jax.experimental import pallas as pl
from jax.experimental.pallas import tpu as pltpu
from jax.sharding import PartitionSpec as P

MINI = 16
EPSILON = 1e-06
ETA_BASE = 0.5
BF = jnp.bfloat16
F32 = jnp.float32


def mm(left, right):
    return lax.dot_general(left, right, (((1,), (0,)), ((), ())), preferred_element_type=F32)


def mm_nt(left, right):
    return lax.dot_general(left, right, (((1,), (1,)), ((), ())), preferred_element_type=F32)


def mm_tn(left, right):
    return lax.dot_general(left, right, (((0,), (0,)), ((), ())), preferred_element_type=F32)


def gelu_parts(value):
    cdf = 0.5 + 0.5 * lax.erf(value * 0.7071067811865476)
    pdf = jnp.exp(-0.5 * value * value) * 0.3989422804014327
    return cdf, pdf


def fwd_kernel(
    kq_ref, kmv_ref, qf_ref, aux_ref, w1i_ref, c1i_ref, w2i_ref, c2i_ref,
    mixed_ref, w1s_ref, w2s_ref, h_ref, r_ref, g1_ref, g2_ref, ga_ref, ug_ref, gp_ref,
    w1_ref, c1_ref, w2_ref, c2_ref, *, unroll,
):
    chains, group = kq_ref.shape[:2]

    @pl.when(pl.program_id(0) == 0)
    def _():
        w1_ref[...] = w1i_ref[...]
        c1_ref[...] = c1i_ref[...]
        w2_ref[...] = w2i_ref[...]
        c2_ref[...] = c2i_ref[...]

    every = range(chains)

    def step(j):
        kq = [kq_ref[i, j] for i in every]
        k = [kq[i][:MINI] for i in every]
        q = [kq[i][MINI:] for i in every]
        aux = [aux_ref[i, j] for i in every]
        mix = [aux[i][:, :MINI] for i in every]
        rate = [aux[i][:, MINI : MINI + 1] for i in every]
        kmv = [kmv_ref[i, j] for i in every]
        qf = [qf_ref[i, j] for i in every]
        w1 = [w1_ref[i] for i in every]
        w2 = [w2_ref[i] for i in every]
        c1 = [c1_ref[i] for i in every]
        c2 = [c2_ref[i] for i in every]
        w1b = [w1[i].astype(BF) for i in every]
        w2b = [w2[i].astype(BF) for i in every]
        both = [mm(kq[i], w1b[i]) + c1[i] for i in every]
        qk = [mm_nt(q[i], k[i]) for i in every]
        parts = [gelu_parts(both[i][:MINI]) for i in every]
        slope = [parts[i][0] + both[i][:MINI] * parts[i][1] for i in every]
        hb = [(both[i][:MINI] * parts[i][0]).astype(BF) for i in every]
        g2 = [mm_nt(hb[i], w2b[i]) + c2[i] + kmv[i] for i in every]
        g2b = [g2[i].astype(BF) for i in every]
        u = [mm(g2b[i], w2b[i]) for i in every]
        fg2 = [rate[i] * g2[i] for i in every]
        w2n = [w2[i] - mm_tn(fg2[i].astype(BF), hb[i]) for i in every]
        c2n = [c2[i] - jnp.sum(fg2[i], axis=0, keepdims=True) for i in every]
        g1 = [u[i] * slope[i] for i in every]
        fg1 = [rate[i] * g1[i] for i in every]
        w1n = [w1[i] - mm_tn(k[i], fg1[i].astype(BF)) for i in every]
        c1n = [c1[i] - jnp.sum(fg1[i], axis=0, keepdims=True) for i in every]
        g1b = [g1[i].astype(BF) for i in every]
        ug = [u[i] * (parts[i][1] * (2.0 - both[i][:MINI] * both[i][:MINI])) for i in every]
        s1 = [(mix[i] * (qk[i] + 1.0)).astype(BF) for i in every]
        pre = [both[i][MINI:] - mm(s1[i], g1b[i]) for i in every]
        parts_q = [gelu_parts(pre[i]) for i in every]
        gp = [parts_q[i][0] + pre[i] * parts_q[i][1] for i in every]
        rb = [(pre[i] * parts_q[i][0]).astype(BF) for i in every]
        s2 = [(mix[i] * (mm_nt(rb[i], hb[i]) + 1.0)).astype(BF) for i in every]
        mixed = [qf[i] + mm_nt(rb[i], w2b[i]) + c2[i] - mm(s2[i], g2b[i]) for i in every]
        for i in every:
            w1s_ref[i, j] = w1b[i]
            w2s_ref[i, j] = w2b[i]
            h_ref[i, j] = hb[i]
            r_ref[i, j] = rb[i]
            g1_ref[i, j] = g1b[i]
            g2_ref[i, j] = g2b[i]
            ga_ref[i, j] = slope[i]
            ug_ref[i, j] = ug[i]
            gp_ref[i, j] = gp[i]
            mixed_ref[i, j] = mixed[i]
            w1_ref[i] = w1n[i]
            w2_ref[i] = w2n[i]
            c1_ref[i] = c1n[i]
            c2_ref[i] = c2n[i]

    def body(turn, _):
        for within in range(unroll):
            step(turn * unroll + within)
        return 0

    lax.fori_loop(0, group // unroll, body, 0)


def bwd_kernel(
    d_ref, kq_ref, aux_ref, w1s_ref, w2s_ref, h_ref, r_ref, g1_ref, g2_ref, ga_ref, ug_ref, gp_ref,
    dq_ref, dk_ref, dv_ref, de_ref, dw1_ref, dc1_ref, dw2_ref, dc2_ref,
    *, unroll,
):
    chains, group = kq_ref.shape[:2]

    @pl.when(pl.program_id(0) == 0)
    def _():
        dw1_ref[...] = jnp.zeros_like(dw1_ref)
        dc1_ref[...] = jnp.zeros_like(dc1_ref)
        dw2_ref[...] = jnp.zeros_like(dw2_ref)
        dc2_ref[...] = jnp.zeros_like(dc2_ref)

    row = lax.broadcasted_iota(jnp.int32, (MINI, MINI), 0)
    col = lax.broadcasted_iota(jnp.int32, (MINI, MINI), 1)
    scale = jnp.where(col <= row, 1.0 / (row + 1).astype(F32), 0.0)
    eye = jnp.where(col == row, 1.0 / MINI, 0.0)

    every = range(chains)

    def step(j):
        def all_of(ref):
            return [ref[i, j] for i in every]

        d, kq, aux = all_of(d_ref), all_of(kq_ref), all_of(aux_ref)
        w1b, w2b, hb, rb, g1b, g2b = (
            all_of(ref) for ref in (w1s_ref, w2s_ref, h_ref, r_ref, g1_ref, g2_ref)
        )
        ga, ug, gp = all_of(ga_ref), all_of(ug_ref), all_of(gp_ref)
        dw1 = [dw1_ref[i] for i in every]
        dw2 = [dw2_ref[i] for i in every]
        dc1 = [dc1_ref[i] for i in every]
        dc2 = [dc2_ref[i] for i in every]
        k = [kq[i][:MINI] for i in every]
        q = [kq[i][MINI:] for i in every]
        mix = [aux[i][:, :MINI] for i in every]
        rate = [aux[i][:, MINI : MINI + 1] for i in every]
        g1 = [g1b[i].astype(F32) for i in every]
        g2 = [g2b[i].astype(F32) for i in every]
        dw1b = [dw1[i].astype(BF) for i in every]
        dw2b = [dw2[i].astype(BF) for i in every]
        t1 = [mm(k[i], dw1b[i]) + dc1[i] for i in every]
        t2 = [mm_nt(hb[i], dw2b[i]) + dc2[i] for i in every]
        db = [d[i].astype(BF) for i in every]
        ds2 = [-mm_nt(db[i], g2b[i]) for i in every]
        x2 = [mm_nt(rb[i], hb[i]) + 1.0 for i in every]
        x1 = [mm_nt(q[i], k[i]) + 1.0 for i in every]
        dx2 = [(ds2[i] * mix[i]).astype(BF) for i in every]
        dr = [mm(db[i], w2b[i]) + mm(dx2[i], hb[i]) for i in every]
        dp = [dr[i] * gp[i] for i in every]
        dpb = [dp[i].astype(BF) for i in every]
        dg1 = [-mm_tn((mix[i] * x1[i]).astype(BF), dpb[i]) - rate[i] * t1[i] for i in every]
        dub = [(dg1[i] * ga[i]).astype(BF) for i in every]
        dg2 = [
            mm_nt(dub[i], w2b[i]) - mm_tn((mix[i] * x2[i]).astype(BF), db[i]) - rate[i] * t2[i]
            for i in every
        ]
        dg2b = [dg2[i].astype(BF) for i in every]
        dh = [
            mm(dg2b[i], w2b[i]) + mm_tn(dx2[i], rb[i]) - mm((rate[i] * g2[i]).astype(BF), dw2b[i])
            for i in every
        ]
        da = [dg1[i] * ug[i] + dh[i] * ga[i] for i in every]
        dab = [da[i].astype(BF) for i in every]
        dw1n = [dw1[i] + mm_tn(kq[i], jnp.concatenate([dab[i], dpb[i]], axis=0)) for i in every]
        dc1n = [dc1[i] + jnp.sum(da[i] + dp[i], axis=0, keepdims=True) for i in every]
        dw2n = [
            dw2[i]
            + mm_tn(
                jnp.concatenate([db[i], dg2b[i], g2b[i]], axis=0),
                jnp.concatenate([rb[i], hb[i], dub[i]], axis=0),
            )
            for i in every
        ]
        dc2n = [dc2[i] + jnp.sum(d[i] + dg2[i], axis=0, keepdims=True) for i in every]
        ds1 = [-mm_nt(dpb[i], g1b[i]) for i in every]
        dx1 = [(ds1[i] * mix[i]).astype(BF) for i in every]
        dq = [d[i] + mm_nt(dpb[i], w1b[i]) + mm(dx1[i], k[i]) for i in every]
        dk = [
            dg2[i]
            - mm_nt((rate[i] * g1[i]).astype(BF), dw1b[i])
            + mm_tn(dx1[i], q[i])
            + mm_nt(dab[i], w1b[i])
            for i in every
        ]
        df = [
            -(
                jnp.sum(g1[i] * t1[i], axis=1, keepdims=True)
                + jnp.sum(g2[i] * t2[i], axis=1, keepdims=True)
            )
            for i in every
        ]
        de = [
            jnp.sum((ds2[i] * x2[i] + ds1[i] * x1[i]) * scale + eye * df[i], axis=0, keepdims=True)
            for i in every
        ]
        for i in every:
            dq_ref[i, j] = dq[i].astype(BF)
            dk_ref[i, j] = dk[i].astype(BF)
            dv_ref[i, j] = (-dg2[i]).astype(BF)
            de_ref[i, j] = de[i]
            dw1_ref[i] = dw1n[i]
            dc1_ref[i] = dc1n[i]
            dw2_ref[i] = dw2n[i]
            dc2_ref[i] = dc2n[i]

    def body(turn, _):
        for within in range(unroll):
            step(group - 1 - (turn * unroll + within))
        return 0

    lax.fori_loop(0, group // unroll, body, 0)


def run_fwd(kq, kmv, qf, aux, w1, c1, w2, c2, group=8, unroll=2):
    chains, count, _, hd = kq.shape
    inner = w1.shape[-1]
    steps = count // group

    def spec(rows, cols):
        return pl.BlockSpec((chains, group, rows, cols), lambda g: (0, g, 0, 0))

    def whole(rows, cols):
        return pl.BlockSpec((chains, rows, cols), lambda g: (0, 0, 0))

    def out(rows, cols, dtype):
        return jax.ShapeDtypeStruct((chains, count, rows, cols), dtype)

    return pl.pallas_call(
        partial(fwd_kernel, unroll=unroll),
        grid=(steps,),
        in_specs=[spec(2 * MINI, hd), spec(MINI, hd), spec(MINI, hd), spec(MINI, 128),
                  whole(hd, inner), whole(1, inner), whole(hd, inner), whole(1, hd)],
        out_specs=[spec(MINI, hd), spec(hd, inner), spec(hd, inner), spec(MINI, inner), spec(MINI, inner),
                   spec(MINI, inner), spec(MINI, hd), spec(MINI, inner), spec(MINI, inner), spec(MINI, inner)],
        out_shape=[out(MINI, hd, F32), out(hd, inner, BF), out(hd, inner, BF), out(MINI, inner, BF), out(MINI, inner, BF),
                   out(MINI, inner, BF), out(MINI, hd, BF), out(MINI, inner, F32), out(MINI, inner, F32), out(MINI, inner, F32)],
        scratch_shapes=[pltpu.VMEM((chains, hd, inner), F32), pltpu.VMEM((chains, 1, inner), F32),
                        pltpu.VMEM((chains, hd, inner), F32), pltpu.VMEM((chains, 1, hd), F32)],
        compiler_params=pltpu.CompilerParams(vmem_limit_bytes=48 << 20),
        cost_estimate=pl.CostEstimate(flops=60_000_000_000, bytes_accessed=40_000_000, transcendentals=0),
        name="chain_forward",
    )(kq, kmv, qf, aux, w1, c1, w2, c2)


def run_bwd(d, kq, aux, saved, group=8, unroll=2):
    chains, count, _, hd = kq.shape
    inner = saved[0].shape[-1]
    steps = count // group

    def spec(rows, cols):
        return pl.BlockSpec((chains, group, rows, cols), lambda g: (0, steps - 1 - g, 0, 0))

    def whole(rows, cols):
        return pl.BlockSpec((chains, rows, cols), lambda g: (0, 0, 0))

    def out(rows, cols, dtype):
        return jax.ShapeDtypeStruct((chains, count, rows, cols), dtype)

    def st(rows, cols):
        return jax.ShapeDtypeStruct((chains, rows, cols), F32)

    return pl.pallas_call(
        partial(bwd_kernel, unroll=unroll),
        grid=(steps,),
        in_specs=[spec(MINI, hd), spec(2 * MINI, hd), spec(MINI, 128), spec(hd, inner), spec(hd, inner),
                  spec(MINI, inner), spec(MINI, inner), spec(MINI, inner), spec(MINI, hd),
                  spec(MINI, inner), spec(MINI, inner), spec(MINI, inner)],
        out_specs=[spec(MINI, hd), spec(MINI, hd), spec(MINI, hd), spec(1, MINI),
                   whole(hd, inner), whole(1, inner), whole(hd, inner), whole(1, hd)],
        out_shape=[out(MINI, hd, BF), out(MINI, hd, BF), out(MINI, hd, BF), out(1, MINI, F32),
                   st(hd, inner), st(1, inner), st(hd, inner), st(1, hd)],
        compiler_params=pltpu.CompilerParams(vmem_limit_bytes=48 << 20),
        cost_estimate=pl.CostEstimate(flops=70_000_000_000, bytes_accessed=40_000_000, transcendentals=0),
        name="chain_backward",
    )(d, kq, aux, *saved)


def gelu(value):
    return jax.nn.gelu(value, approximate=False)


def gelu_slope(value):
    return (
        0.5 * (1.0 + lax.erf(value * 0.7071067811865476))
        + value * jnp.exp(-0.5 * value * value) * 0.3989422804014327
    )


def row_norm(value):
    return lax.rsqrt(jnp.mean(value * value, axis=-1, keepdims=True) + EPSILON)


def pieces_of(chains, depth, head_dim, inner_share, head_share):
    return (
        ("lr", (depth, chains)),
        ("w1", (chains, head_dim, inner_share)),
        ("w2", (chains, head_dim, inner_share)),
        ("b1", (chains, inner_share)),
        ("b2", (chains, head_share)),
        ("pg", (chains, head_share)),
        ("pb", (chains, head_share)),
        ("n1", (depth,)),
        ("n2", (depth,)),
    )


def size_of(shape):
    total = 1
    for extent in shape:
        total *= extent
    return total


def swap(value):
    return lax.ppermute(value, "tp", [(0, 1), (1, 0)])


def spread(value, axis):
    size = lax.axis_size(axis)
    me = lax.axis_index(axis)
    whole = lax.dynamic_update_index_in_dim(
        jnp.zeros((size,) + value.shape, value.dtype), value, me, 0
    )
    for bit in range(1, size):
        piece = lax.ppermute(value, axis, [(source, source ^ bit) for source in range(size)])
        whole = lax.dynamic_update_index_in_dim(whole, piece, me ^ bit, 0)
    return whole


def in_turn(first, second):
    return jnp.where(lax.axis_index("tp") == 0, jnp.stack([first, second]), jnp.stack([second, first]))


def on_device(
    tokens,
    lengths,
    norm1_gain,
    qkv_weight,
    lr_weight,
    inner_w1,
    inner_b1,
    inner_w2,
    inner_b2,
    post_gain,
    post_bias,
    gate_weight,
    out_weight,
    norm2_gain,
    ffn_gate,
    ffn_up,
    ffn_down,
    cotangent,
):
    micro, span, width = tokens.shape
    ring = lax.axis_size("ctx")
    shards = lax.axis_size("shard")
    pair = lax.axis_size("tp")
    place = lax.axis_index("ctx")
    core = lax.axis_index("tp")
    local_heads, head_dim, inner_share = inner_w1.shape
    head_share = inner_b2.shape[1]
    depth = norm1_gain.shape[0]
    inner = inner_share * shards
    total_heads = local_heads * pair
    chains = -(-total_heads // ring)
    span_all = ring * span
    count = span_all // MINI
    cols = chains * head_dim
    wide = 4 * cols

    row_tokens = lax.dynamic_index_in_dim(tokens, core, 0, keepdims=False)
    slot_tokens = spread(row_tokens, "ctx").reshape(span_all, width)

    first_head = jnp.minimum(place * chains, total_heads - chains)
    owner = first_head // local_heads
    local_first = first_head - owner * local_heads

    def of_heads(value, axis):
        return lax.dynamic_slice_in_dim(value, local_first, chains, axis)

    pieces = pieces_of(chains, depth, head_dim, inner_share, head_share)
    small_size = sum(size_of(shape) for _, shape in pieces)
    small_rows = -(-small_size // wide)
    small_rows = -(-(small_rows + depth) // 16) * 16 - depth
    half_rows = (small_rows + depth) // 2
    own = {
        "lr": of_heads(lr_weight, 1),
        "w1": of_heads(inner_w1, 0),
        "w2": of_heads(inner_w2, 0),
        "b1": of_heads(inner_b1, 0),
        "b2": of_heads(inner_b2, 0),
        "pg": of_heads(post_gain, 0),
        "pb": of_heads(post_bias, 0),
        "n1": norm1_gain,
        "n2": norm2_gain,
    }
    small = jnp.concatenate([own[name].reshape(-1) for name, _ in pieces])
    small = jnp.pad(small, (0, small_rows * wide - small_size)).reshape(small_rows, wide)
    qkv_heads = of_heads(qkv_weight.reshape(depth, 3, local_heads, head_dim), 2)
    gate_heads = of_heads(gate_weight.reshape(depth, local_heads, head_dim), 1)
    big = jnp.concatenate(
        [qkv_heads.reshape(depth, 3 * cols), gate_heads.reshape(depth, cols)], axis=1
    )
    packed = jnp.concatenate([big, small], axis=0)
    packed = jnp.where(core == owner, packed, swap(packed))
    packed = spread(lax.dynamic_slice_in_dim(packed, core * half_rows, half_rows, 0), "shard")
    packed = in_turn(packed, swap(packed))
    gathered = packed.transpose(1, 0, 2, 3).reshape(shards, depth + small_rows, wide)
    units = ffn_gate.shape[1]
    half_out = out_weight.shape[0]
    row_pack = jnp.concatenate([ffn_gate, ffn_up, ffn_down.T, out_weight.T], axis=1)
    part = depth // ring
    row_part = lax.dynamic_slice_in_dim(row_pack, place * part, part, 0)
    row_part, gathered = lax.optimization_barrier((row_part, gathered))
    row_part = spread(row_part, "shard")

    w_chain = gathered[:, :depth].reshape(width, wide)
    flat = gathered[:, depth:].reshape(shards, small_rows * wide)
    full = {}
    offset = 0
    for name, shape in pieces:
        full[name] = flat[:, offset : offset + size_of(shape)].reshape((shards,) + shape)
        offset += size_of(shape)
    w_rate = full["lr"].reshape(width, chains)
    gain_one = full["n1"].reshape(width).astype(F32)
    gain_two = full["n2"].reshape(width).astype(F32)

    def along(name):
        return jnp.moveaxis(full[name], 0, -2).reshape(full[name].shape[1:-1] + (-1,)).astype(F32)

    init_first, init_second = along("w1"), along("w2")
    init_first_bias, init_second_bias = along("b1"), along("b2")
    norm_gain, norm_bias = along("pg"), along("pb")

    slot_length = lax.dynamic_index_in_dim(lengths, core, 0, keepdims=False)
    live_all = (lax.iota(jnp.int32, span_all) < slot_length).astype(F32)
    slot_in = slot_tokens.astype(F32)
    unit_in = slot_in * row_norm(slot_in)
    normed_one = (unit_in * gain_one).astype(BF)
    projected = mm(normed_one, w_chain).reshape(span_all, 4, chains, head_dim).transpose(1, 2, 0, 3)
    queries, keys, values, gate_pre = (projected[i] for i in range(4))
    gate_rate = jax.nn.sigmoid(mm(normed_one, w_rate))
    eta = ETA_BASE / head_dim * gate_rate * live_all[:, None]
    eta_blocks = eta.T.reshape(chains, count, MINI)

    def blocks(value):
        return value.reshape(chains, count, MINI, value.shape[-1])

    row_index = lax.broadcasted_iota(jnp.int32, (MINI, MINI), 0)
    col_index = lax.broadcasted_iota(jnp.int32, (MINI, MINI), 1)
    scale = jnp.where(col_index <= row_index, 1.0 / (row_index + 1).astype(F32), 0.0)
    aux = jnp.concatenate(
        [
            scale * eta_blocks[:, :, None, :],
            eta_blocks[..., None] / MINI,
            jnp.zeros((chains, count, MINI, 128 - MINI - 1), F32),
        ],
        axis=-1,
    )
    kq = jnp.concatenate([blocks(keys), blocks(queries)], axis=2).astype(BF)
    kq, row_part = lax.optimization_barrier((kq, row_part))
    row_all = spread(row_part, "ctx")
    forward = run_fwd(
        kq,
        blocks(keys - values),
        blocks(queries),
        aux,
        init_first,
        init_first_bias[:, None],
        init_second,
        init_second_bias[:, None],
    )
    mixed, saved = forward[0].reshape(chains, span_all, head_dim), forward[1:]

    centered = mixed - jnp.mean(mixed, axis=-1, keepdims=True)
    scale_head = lax.rsqrt(jnp.mean(centered * centered, axis=-1, keepdims=True) + EPSILON)
    unit = centered * scale_head
    head_out = unit * norm_gain[:, None] + norm_bias[:, None]
    post_chain = (gelu(gate_pre) * head_out).astype(BF)

    def to_rows(value):
        return lax.all_to_all(value.reshape(ring, span, -1), "ctx", 0, 0)

    post = to_rows(post_chain.transpose(1, 0, 2).reshape(span_all, cols))
    post = post.transpose(1, 0, 2).reshape(span, ring * cols)[:, : total_heads * head_dim]

    w_own = row_all.transpose(1, 0, 2, 3).reshape(width, -1)
    w_other = swap(w_own)

    def split_up(value):
        return tuple(value[:, start : start + units] for start in range(0, 3 * units, units))

    halves = (split_up(w_own), split_up(w_other))
    w_out = jnp.concatenate(
        [
            jnp.where(core == 0, w_own[:, 3 * units :], w_other[:, 3 * units :]),
            jnp.where(core == 0, w_other[:, 3 * units :], w_own[:, 3 * units :]),
        ],
        axis=1,
    )
    row_in = row_tokens.astype(F32)
    hidden = row_in + mm_nt(post, w_out)
    scale_two = row_norm(hidden)
    normed_two = (hidden * scale_two * gain_two).astype(BF)
    position = place * span + lax.iota(jnp.int32, span)
    live = (position < slot_length).astype(F32)[:, None]
    cot = lax.dynamic_index_in_dim(cotangent, core, 0, keepdims=False)
    back = cot.astype(F32) * live
    back_low = back.astype(BF)
    feed = 0.0
    grad_two = 0.0
    sums = []
    for w_gate, w_up, w_down in halves:
        up_gate = mm(normed_two, w_gate)
        up_lin = mm(normed_two, w_up)
        gate = jax.nn.sigmoid(up_gate)
        act_low = (up_gate * gate * up_lin).astype(BF)
        feed = feed + mm_nt(act_low, w_down)
        grad_act = mm(back_low, w_down)
        grad_gate_low = (grad_act * up_lin * gate * (1.0 + up_gate * (1.0 - gate))).astype(BF)
        grad_lin_low = (grad_act * up_gate * gate).astype(BF)
        grad_two = grad_two + mm_nt(grad_gate_low, w_gate) + mm_nt(grad_lin_low, w_up)
        sums.append(
            [
                mm_tn(normed_two, grad_gate_low),
                mm_tn(normed_two, grad_lin_low),
                mm_tn(back_low, act_low),
            ]
        )
    output = (hidden + feed).astype(BF)
    lifted = grad_two * gain_two
    grad_hidden = (
        back
        + scale_two * lifted
        - hidden * scale_two**3 * jnp.mean(lifted * hidden, axis=-1, keepdims=True)
    )
    grad_gain_two = jnp.sum(grad_two * hidden * scale_two, axis=0)
    grad_hidden_low = grad_hidden.astype(BF)
    grad_post = mm(grad_hidden_low, w_out)

    grad_out = mm_tn(grad_hidden_low, post)
    grad_out_own = lax.dynamic_slice_in_dim(grad_out, core * half_out, half_out, 1)
    grad_out_other = lax.dynamic_slice_in_dim(grad_out, (1 - core) * half_out, half_out, 1)
    own_sum = jnp.concatenate(sums[0] + [grad_out_own], axis=1)
    other_sum = jnp.concatenate(sums[1] + [grad_out_other], axis=1).astype(BF)
    row_sum = (own_sum + swap(other_sum).astype(F32)).astype(BF)
    row_sum = lax.all_to_all(row_sum.reshape(shards * ring, part, -1), ("shard", "ctx"), 0, 0)

    grad_post = jnp.pad(grad_post.astype(BF), ((0, 0), (0, ring * cols - total_heads * head_dim)))
    grad_post = lax.all_to_all(grad_post.reshape(span, ring, cols).transpose(1, 0, 2), "ctx", 0, 0)
    grad_post = grad_post.reshape(span_all, chains, head_dim).transpose(1, 0, 2).astype(F32)
    grad_gate_pre = (grad_post * gelu_slope(gate_pre) * head_out).astype(BF)
    grad_head = grad_post * gelu(gate_pre)
    grad_norm_gain = jnp.sum(grad_head * unit, axis=1)
    grad_norm_bias = jnp.sum(grad_head, axis=1)
    lifted = grad_head * norm_gain[:, None]
    grad_mixed = scale_head * (
        lifted
        - jnp.mean(lifted, axis=-1, keepdims=True)
        - unit * jnp.mean(lifted * unit, axis=-1, keepdims=True)
    )
    grad_q, grad_k, grad_v, grad_eta, d_first, d_first_bias, d_second, d_second_bias = run_bwd(
        blocks(grad_mixed), kq, aux, saved
    )
    grad_eta = grad_eta.reshape(chains, span_all).T
    grad_rate = grad_eta * (ETA_BASE / head_dim) * gate_rate * (1.0 - gate_rate) * live_all[:, None]
    grad_rate_low = grad_rate.astype(BF)
    grad_all = jnp.stack(
        [value.reshape(chains, span_all, head_dim) for value in (grad_q, grad_k, grad_v, grad_gate_pre)]
    )
    grad_all = grad_all.transpose(2, 0, 1, 3).reshape(span_all, wide)
    back_part = mm_nt(grad_all, w_chain) + mm_nt(grad_rate_low, w_rate)
    grad_gain_one = jnp.sum(back_part * unit_in, axis=0)
    back_one = jnp.sum(to_rows(back_part.astype(BF)).astype(F32), axis=0)
    scale_one = row_norm(row_in)
    lifted = back_one * gain_one
    input_grad = (
        grad_hidden
        + scale_one * lifted
        - row_in * scale_one**3 * jnp.mean(lifted * row_in, axis=-1, keepdims=True)
    ).astype(BF)

    row_sum = spread(jnp.sum(row_sum.astype(F32), axis=0).astype(BF), "ctx")
    row_sum = row_sum.reshape(depth, -1).astype(F32)
    g_ffn_gate = row_sum[:, :units]
    g_ffn_up = row_sum[:, units : 2 * units]
    g_ffn_down = row_sum[:, 2 * units : 3 * units].T
    g_out = row_sum[:, 3 * units :].T

    grad_big = mm_tn(normed_one, grad_all)
    grad_lr = mm_tn(normed_one, grad_rate_low)

    def by_shard(value):
        split = value.reshape(value.shape[:-1] + (shards, -1))
        return jnp.moveaxis(split, -2, 0).reshape(shards, -1)

    flat = jnp.concatenate(
        [
            grad_lr.reshape(shards, -1),
            by_shard(d_first),
            by_shard(d_second),
            by_shard(d_first_bias),
            by_shard(d_second_bias),
            by_shard(grad_norm_gain),
            by_shard(grad_norm_bias),
            grad_gain_one.reshape(shards, -1),
            grad_gain_two.reshape(shards, -1),
        ],
        axis=1,
    )
    flat = jnp.pad(flat, ((0, 0), (0, small_rows * wide - small_size)))
    chain_sum = jnp.concatenate(
        [grad_big.reshape(shards, depth, wide), flat.reshape(shards, small_rows, wide)], axis=1
    ).astype(BF)
    kept_half = lax.dynamic_slice_in_dim(chain_sum, core * half_rows, half_rows, 1)
    sent_half = lax.dynamic_slice_in_dim(chain_sum, (1 - core) * half_rows, half_rows, 1)
    chain_sum = (kept_half.astype(F32) + swap(sent_half).astype(F32)).astype(BF)
    chain_sum = lax.all_to_all(chain_sum, "shard", 0, 0)
    chain_sum = spread(jnp.sum(chain_sum.astype(F32), axis=0).astype(BF), "ctx")
    chain_sum = in_turn(chain_sum, swap(chain_sum)).astype(F32)
    chain_sum = chain_sum.transpose(1, 0, 2, 3).reshape(ring, depth + small_rows, wide)
    places = local_heads // chains
    mine = lax.dynamic_slice_in_dim(chain_sum, core * places, places, 0)
    mine_big = mine[:, :depth].reshape(places, depth, 4, cols).transpose(1, 2, 0, 3)
    mine_big = mine_big.reshape(depth, 4, local_heads * head_dim)
    flat_all = chain_sum[:, depth:].reshape(ring, -1)
    flat_mine = mine[:, depth:].reshape(places, -1)
    parts = {}
    offset = 0
    for name, shape in pieces:
        source = flat_all if name in ("n1", "n2") else flat_mine
        parts[name] = source[:, offset : offset + size_of(shape)].reshape((source.shape[0],) + shape)
        offset += size_of(shape)

    def stacked(name):
        return parts[name].reshape((local_heads,) + parts[name].shape[2:])

    return (
        in_turn(output, swap(output)),
        in_turn(input_grad, swap(input_grad)),
        jnp.sum(parts["n1"], axis=0),
        mine_big[:, :3],
        parts["lr"].transpose(1, 0, 2).reshape(depth, local_heads),
        stacked("w1"),
        stacked("b1"),
        stacked("w2"),
        stacked("b2"),
        stacked("pg"),
        stacked("pb"),
        mine_big[:, 3],
        g_out,
        jnp.sum(parts["n2"], axis=0),
        g_ffn_gate,
        g_ffn_up,
        g_ffn_down,
    )


def solution(mesh):
    in_specs = (
        P("shard", "ctx", None),
        P("shard"),
        P("shard"),
        P("shard", None, "tp"),
        P("shard", "tp"),
        P("tp", None, "shard"),
        P("tp", "shard"),
        P("tp", None, "shard"),
        P("tp", "shard"),
        P("tp", "shard"),
        P("tp", "shard"),
        P("shard", "tp"),
        P("tp", "shard"),
        P("shard"),
        P("shard", "tp"),
        P("shard", "tp"),
        P("tp", "shard"),
        P("shard", "ctx", None),
    )
    out_specs = (
        P("shard", "ctx", None),
        P("shard", "ctx", None),
        P("shard"),
        P("shard", None, "tp"),
        P("shard", "tp"),
        P("tp", None, "shard"),
        P("tp", "shard"),
        P("tp", None, "shard"),
        P("tp", "shard"),
        P("tp", "shard"),
        P("tp", "shard"),
        P("shard", "tp"),
        P("tp", "shard"),
        P("shard"),
        P("shard", "tp"),
        P("shard", "tp"),
        P("tp", "shard"),
    )
    return jax.shard_map(
        on_device, mesh=mesh, in_specs=in_specs, out_specs=out_specs, check_vma=False
    )
```

time: 5460 us -> 597 us (0.11)
  waiting for transfers between devices: 2380 us -> 187 us
  matrix products: 1440 us -> 53.5 us
  starting transfers between devices: 863 us -> 48.4 us
  local copies, waits for them, and re-layouts: 298 us -> 104 us
  blocking collectives: 165 us -> 0 us
  other arithmetic: 211 us -> 56.9 us
  Pallas kernels: 0 us -> 137 us
    dot_general x1365 -> x27, matrix products: 1440 us -> 53.5 us  [the longest x9 19 us: mm(): lax.dot_general(left, right, (((1,), (0,)), ((), ())), preferred_element_...]
    ppermute x10 -> x26, waiting for transfers between devices: 1070 us -> 116 us  [the longest x18 116 us: spread(): lax.ppermute(value, axis, [(source, source ^ bit) for source in range(siz...]
    ppermute x10 -> x26, starting transfers between devices: 862 us -> 22.9 us  [the longest x18 21.5 us: spread(): lax.ppermute(value, axis, [(source, source ^ bit) for source in range(siz...]
    unnamed x28 -> x0, waiting for transfers between devices: 752 us -> none
    reduce_scatter x6 -> x0, waiting for transfers between devices: 316 us -> none  [the longest x1 68.9 us: on_device(): lax.psum_scatter(g_qkv, 'shard', scatter_dimension=0, tiled=True)]
    psum x4 -> x0, waiting for transfers between devices: 142 us -> none  [the longest x1 81.5 us: on_device(): lax.psum((shares[0], shares[1], shares[2], shares[3], shares[4], shares[5...]
    pallas_call x0 -> x2, Pallas kernels: none -> 137 us  [the longest x1 69.1 us: run_fwd(): pl.pallas_call(partial(fwd_kernel, unroll=unroll), grid=(steps,), in_spec...]
    all_gather x9 -> x0, blocking collectives: 130 us -> none  [the longest x1 23.1 us: on_device(): lax.all_gather(inner_w1, 'shard', axis=2, tiled=True)]
  transfers between devices with their start and end apart: 31 -> 31, of which waited for: 30 -> 13; matrix products, arithmetic and copies ran while one was open for 3% -> 27% of each run, Pallas kernels for 0% -> 23%
where the time goes in v1:
time: 597 us; the launch traced here: 590 us
  waiting for transfers between devices  187 us (31%)
  Pallas kernels  137 us (23%)
  local copies, waits for them, and re-layouts  104 us (17%)
  other arithmetic  56.9 us (10%)
  matrix products  53.5 us (9%)
  starting transfers between devices  48.4 us (8%)
    ppermute x18, waiting for transfers between devices, spread(): lax.ppermute(value, axis, [(source, source ^ bit) for source in range(siz...  116 us
    pallas_call x1, Pallas kernels, run_fwd(): pl.pallas_call(partial(fwd_kernel, unroll=unroll), grid=(steps,), in_spec...  69.1 us
    pallas_call x1, Pallas kernels, run_bwd(): pl.pallas_call(partial(bwd_kernel, unroll=unroll), grid=(steps,), in_spec...  68.1 us
    all_to_all x1, waiting for transfers between devices, on_device(): lax.all_to_all(row_sum.reshape(shards * ring, part, -1), ('shard', 'ctx')...  60.8 us
    ppermute x18, starting transfers between devices, spread(): lax.ppermute(value, axis, [(source, source ^ bit) for source in range(siz...  21.5 us
    dot_general x9, matrix products, mm(): lax.dot_general(left, right, (((1,), (0,)), ((), ())), preferred_element_...  19 us
    dot_general x9, matrix products, mm_nt(): lax.dot_general(left, right, (((1,), (1,)), ((), ())), preferred_element_...  18.4 us
    convert_element_type x18, local copies, waits for them, and re-layouts, along(): jnp.moveaxis(full[name], 0, -2).reshape(full[name].shape[1:-1] + (-1,))  16.9 us
  transfers between devices with their start and end apart: 31, of which 13 were waited for; matrix products, arithmetic and copies ran while one was open for 27% of the time, Pallas kernels for 23%

profile of v1, /device:TPU:12, one launch (start us, length us, event | category | flops | bytes accessed | tf_op | source)
XLA Modules:
  0.0 589.8 jit_solution(14117752691418775153)
XLA Ops:
  23.3 4.4 collective-permute-done.4
  29.4 6.0 %collective-permute-done.5 = bf16[120,768]{0,1:T(8,128)(2,1)} collective-permute-done((bf16[120,768]{0,1:T(8,128)(2,1)S(1)}, bf16[120,768]{0,1:T(8,128)(2,1)}, u32[]{:S(2)}, u32[]{:S(2)}) %collective-permute-start.5) | collective-permute-done | bytes 184352 | tf_op jit(solution)/shard_map/ppermute | solution.py:339
  36.5 3.3 collective-permute-done.6
  69.3 8.2 %collective-permute-done.9 = bf16[48,3456]{1,0:T(8,128)(2,1)} collective-permute-done((bf16[48,3456]{1,0:T(8,128)(2,1)}, bf16[48,3456]{1,0:T(8,128)(2,1)}, u32[]{:S(2)}, u32[]{:S(2)}) %collective-permute-start.9) | collective-permute-done | bytes 331808 | tf_op jit(solution)/shard_map/ppermute | solution.py:339
  79.3 5.5 collective-permute-done.10
  122.9 49.2 %collective-permute-done.12 = bf16[4,48,3456]{2,1,0:T(8,128)(2,1)S(1)} collective-permute-done((bf16[4,48,3456]{2,1,0:T(8,128)(2,1)}, bf16[4,48,3456]{2,1,0:T(8,128)(2,1)S(1)}, u32[]{:S(2)}, u32[]{:S(2)}) %collective-permute-start.12) | collective-permute-done | bytes 1327136 | tf_op jit(solution)/shard_map/ppermute | solution.py:339
  174.5 69.1 %chain_forward.1 = (f32[3,64,16,64]{3,2,1,0:T(8,128)S(1)}, bf16[3,64,64,256]{3,2,1,0:T(8,128)(2,1)}, bf16[3,64,64,256]{3,2,1,0:T(8,128)(2,1)}, bf16[3,64,16,256]...) custom-call(bf16[3,64,32,64]{3,2,1,0:T(8,128)(2,1)} %pad_maximum_fus, ...), custom_call_target="tpu_custom_call" | custom-call | flops 60000002048 | bytes 40000000 | tf_op jit(solution)/shard_map/chain_forward/pallas_call | solution.py:242
  249.0 3.9 fusion.72
  254.0 3.8 all-to-all-start
  267.6 3.2 multiply_convert_fusion.5
  295.1 4.2 all-to-all-start.1
  308.4 3.3 multiply_reduce_fusion.4
  313.6 68.1 %chain_backward.1 = (bf16[3,64,16,64]{3,2,1,0:T(8,128)(2,1)S(1)}, bf16[3,64,16,64]{3,2,1,0:T(8,128)(2,1)S(1)}, bf16[3,64,16,64]{3,2,1,0:T(8,128)(2,1)S(1)}, f32[...) custom-call(f32[3,64,16,64]{3,2,1,0:T(8,128)S(1)} %bitcast.247, ...), custom_call_target="tpu_custom_call" | custom-call | flops 70000001024 | bytes 40000000 | tf_op jit(solution)/shard_map/chain_backward/pallas_call | solution.py:276
  392.3 4.8 all-to-all-start.2
  418.8 4.3 all-to-all-start.3
  423.0 8.0 %fusion = bf16[768,3456]{1,0:T(8,128)(2,1)} fusion(f32[768,384]{1,0:T(8,128)} %constant_dynamic-slice_fusion, f32[768,1024]{1,0:T(8,128)S(1)} %copy-done.13, f32[768,1024]{1,0:T(8,128)} %fusion.99, f32[768,1024]{1,0:T(8,128)} %fusion.98, bf16[768,3456]{1,0:T(8,128)(2,1)} %collective-permute-done.22), kind=kLoop, calls=%fused_computation.1 | loop fusion | flops 15925248 | bytes 21233664 | tf_op jit(solution)/shard_map/convert_element_type | solution.py:560
  431.1 8.4 %all-to-all-done.3 = bf16[4,120,768]{2,1,0:T(8,128)(2,1)} async-done(((bf16[4,120,768]{2,1,0:T(8,128)(2,1)}), bf16[4,120,768]{2,1,0:T(8,128)(2,1)}, u32[]{:S(2)}, u32[]{:S(2)}) %all-to-all-start.3) | async-done | bytes 737312 | tf_op jit(solution)/shard_map/all_to_all | solution.py:632
  439.5 8.4 %all-to-all-start.4 = ((bf16[16,48,3456]{2,1,0:T(8,128)(2,1)}), bf16[16,48,3456]{2,1,0:T(8,128)(2,1)}, u32[]{:S(2)}, u32[]{:S(2)}) async-start(bf16[16,48,3456]{2,1,0:T(8,128)(2,1)} %bitcast.251), calls=%async_computation.4 | async-start | bytes 10616832 | tf_op jit(solution)/shard_map/all_to_all | solution.py:561
  459.2 10.8 %collective-permute-done.18 = bf16[120,768]{1,0:T(8,128)(2,1)S(1)} collective-permute-done((bf16[120,768]{1,0:T(8,128)(2,1)S(1)}, bf16[120,768]{1,0:T(8,128)(2,1)S(1)}, u32[]{:S(2)}, u32[]{:S(2)}) %collective-permute-start.18) | collective-permute-done | bytes 184352 | tf_op jit(solution)/shard_map/ppermute | solution.py:339
  469.9 14.8 %collective-permute-done.19 = bf16[120,768]{1,0:T(8,128)(2,1)S(1)} collective-permute-done((bf16[120,768]{1,0:T(8,128)(2,1)S(1)}, bf16[120,768]{1,0:T(8,128)(2,1)S(1)}, u32[]{:S(2)}, u32[]{:S(2)}) %collective-permute-start.19) | collective-permute-done | bytes 184352 | tf_op jit(solution)/shard_map/ppermute | solution.py:339
  505.1 60.8 %all-to-all-done.4 = bf16[16,48,3456]{2,1,0:T(8,128)(2,1)} async-done(((bf16[16,48,3456]{2,1,0:T(8,128)(2,1)}), bf16[16,48,3456]{2,1,0:T(8,128)(2,1)}, u32[]{:S(2)}, u32[]{:S(2)}) %all-to-all-start.4) | async-done | bytes 5308448 | tf_op jit(solution)/shard_map/all_to_all | solution.py:561
  565.9 3.4 reduce_sum.184
  573.1 7.0 %collective-permute-done.23 = bf16[48,3456]{1,0:T(8,128)(2,1)S(1)} collective-permute-done((bf16[48,3456]{1,0:T(8,128)(2,1)S(1)}, bf16[48,3456]{1,0:T(8,128)(2,1)S(1)}, u32[]{:S(2)}, u32[]{:S(2)}) %collective-permute-start.23) | collective-permute-done | bytes 331808 | tf_op jit(solution)/shard_map/ppermute | solution.py:339
  580.2 6.8 %collective-permute-done.24 = bf16[48,3456]{1,0:T(8,128)(2,1)S(1)} collective-permute-done((bf16[48,3456]{1,0:T(8,128)(2,1)S(1)}, bf16[48,3456]{1,0:T(8,128)(2,1)S(1)}, u32[]{:S(2)}, u32[]{:S(2)}) %collective-permute-start.24) | collective-permute-done | bytes 331808 | tf_op jit(solution)/shard_map/ppermute | solution.py:339
  (455 shorter events, 217.7 us)
Async XLA Ops:
  1.9 19.9 %collective-permute-start = (bf16[256,768]{1,0:T(8,128)(2,1)S(1)}, bf16[256,768]{1,0:T(8,128)(2,1)}, u32[]{:S(2)}, u32[]{:S(2)}) collective-permute-start(bf16[256,768]{1,0:T(8,128)(2,1)S(1)} %get-tuple-element.94), channel_id=1, source_target_pairs={{0,2},{2,0},{4,6},{6,4},{1,3},{3,1},{5,7},{7,5},{8,10},{10,8},{12,... | collective-permute-start | bytes 1179656 | tf_op jit(solution)/shard_map/ppermute | solution.py:339
  3.4 36.6 %collective-permute-start.1 = (bf16[256,768]{1,0:T(8,128)(2,1)S(1)}, bf16[256,768]{1,0:T(8,128)(2,1)}, u32[]{:S(2)}, u32[]{:S(2)}) collective-permute-start(bf16[256,768]{1,0:T(8,128)(2,1)S(1)} %get-tuple-element.94), channel_id=1, source_target_pairs={{0,4},{2,6},{4,0},{6,2},{1,5},{3,7},{5,1},{7,3},{8,12},{10,14},{12... | collective-permute-start | bytes 1179656 | tf_op jit(solution)/shard_map/ppermute | solution.py:339
  3.9 37.1 %collective-permute-start.2 = (bf16[256,768]{1,0:T(8,128)(2,1)S(1)}, bf16[256,768]{1,0:T(8,128)(2,1)}, u32[]{:S(2)}, u32[]{:S(2)}) collective-permute-start(bf16[256,768]{1,0:T(8,128)(2,1)S(1)} %get-tuple-element.94), channel_id=1, source_target_pairs={{0,6},{2,4},{4,2},{6,0},{1,7},{3,5},{5,3},{7,1},{8,14},{10,12},{12... | collective-permute-start | bytes 1179656 | tf_op jit(solution)/shard_map/ppermute | solution.py:339
  19.1 16.3 %collective-permute-start.5 = (bf16[120,768]{0,1:T(8,128)(2,1)S(1)}, bf16[120,768]{0,1:T(8,128)(2,1)}, u32[]{:S(2)}, u32[]{:S(2)}) collective-permute-start(bf16[120,768]{0,1:T(8,128)(2,1)S(1)} %dynamic-slice_select_fusion), channel_id=1, source_target_pairs={{0,16},{8,24},{16,0},{24,8},{1,17},{9,25},{17,1},{25,9},{2,18},{10... | collective-permute-start | bytes 552968 | tf_op jit(solution)/shard_map/ppermute | solution.py:339
  21.8 18.0 %collective-permute-start.6 = (bf16[120,768]{0,1:T(8,128)(2,1)S(1)}, bf16[120,768]{0,1:T(8,128)(2,1)S(1)}, u32[]{:S(2)}, u32[]{:S(2)}) collective-permute-start(bf16[120,768]{0,1:T(8,128)(2,1)S(1)} %dynamic-slice_select_fusion), channel_id=1, source_target_pairs={{0,24},{8,16},{16,8},{24,0},{1,25},{9,17},{17,9},{25,1},{2,26},{10... | collective-permute-start | bytes 552968 | tf_op jit(solution)/shard_map/ppermute | solution.py:339
  51.7 15.8 %collective-permute-start.8 = (bf16[48,3456]{1,0:T(8,128)(2,1)}, bf16[48,3456]{1,0:T(8,128)(2,1)}, u32[]{:S(2)}, u32[]{:S(2)}) collective-permute-start(bf16[48,3456]{1,0:T(8,128)(2,1)} %fusion.76), channel_id=1, source_target_pairs={{0,8},{8,0},{16,24},{24,16},{1,9},{9,1},{17,25},{25,17},{2,10},{10... | collective-permute-start | bytes 995336 | tf_op jit(solution)/shard_map/ppermute | solution.py:339
  51.8 25.8 %collective-permute-start.9 = (bf16[48,3456]{1,0:T(8,128)(2,1)}, bf16[48,3456]{1,0:T(8,128)(2,1)}, u32[]{:S(2)}, u32[]{:S(2)}) collective-permute-start(bf16[48,3456]{1,0:T(8,128)(2,1)} %fusion.76), channel_id=1, source_target_pairs={{0,16},{8,24},{16,0},{24,8},{1,17},{9,25},{17,1},{25,9},{2,18},{10... | collective-permute-start | bytes 995336 | tf_op jit(solution)/shard_map/ppermute | solution.py:339
  54.8 30.0 %collective-permute-start.10 = (bf16[48,3456]{1,0:T(8,128)(2,1)}, bf16[48,3456]{1,0:T(8,128)(2,1)}, u32[]{:S(2)}, u32[]{:S(2)}) collective-permute-start(bf16[48,3456]{1,0:T(8,128)(2,1)} %fusion.76), channel_id=1, source_target_pairs={{0,24},{8,16},{16,8},{24,0},{1,25},{9,17},{17,9},{25,1},{2,26},{10... | collective-permute-start | bytes 995336 | tf_op jit(solution)/shard_map/ppermute | solution.py:339
  86.6 33.9 %collective-permute-start.11 = (bf16[4,48,3456]{2,1,0:T(8,128)(2,1)}, bf16[4,48,3456]{2,1,0:T(8,128)(2,1)}, u32[]{:S(2)}, u32[]{:S(2)}) collective-permute-start(bf16[4,48,3456]{2,1,0:T(8,128)(2,1)} %bitcast_dynamic-update-slice_fusion.11), channel_id=1, source_target_pairs={{0,2},{2,0},{4,6},{6,4},{1,3},{3,1},{5,7},{7,5},{8,10},{10,8},{12,... | collective-permute-start | bytes 3981320 | tf_op jit(solution)/shard_map/ppermute | solution.py:339
  113.3 58.8 %collective-permute-start.12 = (bf16[4,48,3456]{2,1,0:T(8,128)(2,1)}, bf16[4,48,3456]{2,1,0:T(8,128)(2,1)S(1)}, u32[]{:S(2)}, u32[]{:S(2)}) collective-permute-start(bf16[4,48,3456]{2,1,0:T(8,128)(2,1)} %bitcast_dynamic-update-slice_fusion.11), channel_id=1, source_target_pairs={{0,4},{2,6},{4,0},{6,2},{1,5},{3,7},{5,1},{7,3},{8,12},{10,14},{12... | collective-permute-start | bytes 3981320 | tf_op jit(solution)/shard_map/ppermute | solution.py:339
  113.8 59.4 %collective-permute-start.13 = (bf16[4,48,3456]{2,1,0:T(8,128)(2,1)}, bf16[4,48,3456]{2,1,0:T(8,128)(2,1)S(1)}, u32[]{:S(2)}, u32[]{:S(2)}) collective-permute-start(bf16[4,48,3456]{2,1,0:T(8,128)(2,1)} %bitcast_dynamic-update-slice_fusion.11), channel_id=1, source_target_pairs={{0,6},{2,4},{4,2},{6,0},{1,7},{3,5},{5,3},{7,1},{8,14},{10,12},{12... | collective-permute-start | bytes 3981320 | tf_op jit(solution)/shard_map/ppermute | solution.py:339
  174.5 86.3 %collective-permute-start.14 = (bf16[768,3456]{1,0:T(8,128)(2,1)}, bf16[768,3456]{1,0:T(8,128)(2,1)}, u32[]{:S(2)}, u32[]{:S(2)}) collective-permute-start(bf16[768,3456]{1,0:T(8,128)(2,1)} %bitcast.53), channel_id=1, source_target_pairs={{0,1},{1,0},{2,3},{3,2},{4,5},{5,4},{6,7},{7,6},{8,9},{9,8},{10,11... | collective-permute-start | bytes 15925256 | tf_op jit(solution)/shard_map/ppermute | solution.py:329
  295.1 12.2 %all-to-all-start.1 = ((bf16[4,256,192]{1,2,0:T(8,128)(2,1)}), bf16[4,256,192]{1,2,0:T(8,128)(2,1)S(1)}, u32[]{:S(2)}, u32[]{:S(2)}) async-start(bf16[4,256,192]{1,2,0:T(8,128)(2,1)} %bitcast.59), calls=%async_computation.1 | async-start | bytes 786432 | tf_op jit(solution)/shard_map/all_to_all | solution.py:564
  304.9 118.1 %collective-permute-start.22 = (bf16[768,3456]{1,0:T(8,128)(2,1)}, bf16[768,3456]{1,0:T(8,128)(2,1)}, u32[]{:S(2)}, u32[]{:S(2)}) collective-permute-start(bf16[768,3456]{1,0:T(8,128)(2,1)} %pad_maximum_fusion), channel_id=1, source_target_pairs={{0,1},{1,0},{2,3},{3,2},{4,5},{5,4},{6,7},{7,6},{8,9},{9,8},{10,11... | collective-permute-start | bytes 15925256 | tf_op jit(solution)/shard_map/ppermute | solution.py:329
  392.3 26.5 %all-to-all-start.2 = ((bf16[4,256,768]{2,1,0:T(8,128)(2,1)}), bf16[4,256,768]{2,1,0:T(8,128)(2,1)}, u32[]{:S(2)}, u32[]{:S(2)}) async-start(bf16[4,256,768]{2,1,0:T(8,128)(2,1)} %bitcast.69), calls=%async_computation.2 | async-start | bytes 3145728 | tf_op jit(solution)/shard_map/all_to_all | solution.py:496
  418.8 20.8 %all-to-all-start.3 = ((bf16[4,120,768]{2,1,0:T(8,128)(2,1)}), bf16[4,120,768]{2,1,0:T(8,128)(2,1)}, u32[]{:S(2)}, u32[]{:S(2)}) async-start(bf16[4,120,768]{2,1,0:T(8,128)(2,1)} %add_convert_fusion), calls=%async_computation.3 | async-start | bytes 1474560 | tf_op jit(solution)/shard_map/all_to_all | solution.py:632
  439.5 126.3 %all-to-all-start.4 = ((bf16[16,48,3456]{2,1,0:T(8,128)(2,1)}), bf16[16,48,3456]{2,1,0:T(8,128)(2,1)}, u32[]{:S(2)}, u32[]{:S(2)}) async-start(bf16[16,48,3456]{2,1,0:T(8,128)(2,1)} %bitcast.251), calls=%async_computation.4 | async-start | bytes 10616832 | tf_op jit(solution)/shard_map/all_to_all | solution.py:561
  452.1 33.6 %collective-permute-start.15 = (bf16[256,768]{1,0:T(8,128)(2,1)S(1)}, bf16[256,768]{1,0:T(8,128)(2,1)}, u32[]{:S(2)}, u32[]{:S(2)}) collective-permute-start(bf16[256,768]{1,0:T(8,128)(2,1)S(1)} %fusion.40), channel_id=1, source_target_pairs={{0,1},{1,0},{2,3},{3,2},{4,5},{5,4},{6,7},{7,6},{8,9},{9,8},{10,11... | collective-permute-start | bytes 1179656 | tf_op jit(solution)/shard_map/ppermute | solution.py:329
  455.5 14.4 %collective-permute-start.18 = (bf16[120,768]{1,0:T(8,128)(2,1)S(1)}, bf16[120,768]{1,0:T(8,128)(2,1)S(1)}, u32[]{:S(2)}, u32[]{:S(2)}) collective-permute-start(bf16[120,768]{1,0:T(8,128)(2,1)S(1)} %reduce_sum.182), channel_id=1, source_target_pairs={{0,2},{2,0},{4,6},{6,4},{1,3},{3,1},{5,7},{7,5},{8,10},{10,8},{12,... | collective-permute-start | bytes 552968 | tf_op jit(solution)/shard_map/ppermute | solution.py:339
  457.0 27.7 %collective-permute-start.19 = (bf16[120,768]{1,0:T(8,128)(2,1)S(1)}, bf16[120,768]{1,0:T(8,128)(2,1)S(1)}, u32[]{:S(2)}, u32[]{:S(2)}) collective-permute-start(bf16[120,768]{1,0:T(8,128)(2,1)S(1)} %reduce_sum.182), channel_id=1, source_target_pairs={{0,4},{2,6},{4,0},{6,2},{1,5},{3,7},{5,1},{7,3},{8,12},{10,14},{12... | collective-permute-start | bytes 552968 | tf_op jit(solution)/shard_map/ppermute | solution.py:339
  457.6 27.1 %collective-permute-start.20 = (bf16[120,768]{1,0:T(8,128)(2,1)S(1)}, bf16[120,768]{1,0:T(8,128)(2,1)S(1)}, u32[]{:S(2)}, u32[]{:S(2)}) collective-permute-start(bf16[120,768]{1,0:T(8,128)(2,1)S(1)} %reduce_sum.182), channel_id=1, source_target_pairs={{0,6},{2,4},{4,2},{6,0},{1,7},{3,5},{5,3},{7,1},{8,14},{10,12},{12... | collective-permute-start | bytes 552968 | tf_op jit(solution)/shard_map/ppermute | solution.py:339
  569.2 10.9 %collective-permute-start.23 = (bf16[48,3456]{1,0:T(8,128)(2,1)S(1)}, bf16[48,3456]{1,0:T(8,128)(2,1)S(1)}, u32[]{:S(2)}, u32[]{:S(2)}) collective-permute-start(bf16[48,3456]{1,0:T(8,128)(2,1)S(1)} %reduce_sum.184), channel_id=1, source_target_pairs={{0,2},{2,0},{4,6},{6,4},{1,3},{3,1},{5,7},{7,5},{8,10},{10,8},{12,... | collective-permute-start | bytes 995336 | tf_op jit(solution)/shard_map/ppermute | solution.py:339
  571.4 15.6 %collective-permute-start.24 = (bf16[48,3456]{1,0:T(8,128)(2,1)S(1)}, bf16[48,3456]{1,0:T(8,128)(2,1)S(1)}, u32[]{:S(2)}, u32[]{:S(2)}) collective-permute-start(bf16[48,3456]{1,0:T(8,128)(2,1)S(1)} %reduce_sum.184), channel_id=1, source_target_pairs={{0,4},{2,6},{4,0},{6,2},{1,5},{3,7},{5,1},{7,3},{8,12},{10,14},{12... | collective-permute-start | bytes 995336 | tf_op jit(solution)/shard_map/ppermute | solution.py:339
  571.4 15.6 %collective-permute-start.25 = (bf16[48,3456]{1,0:T(8,128)(2,1)S(1)}, bf16[48,3456]{1,0:T(8,128)(2,1)S(1)}, u32[]{:S(2)}, u32[]{:S(2)}) collective-permute-start(bf16[48,3456]{1,0:T(8,128)(2,1)S(1)} %reduce_sum.184), channel_id=1, source_target_pairs={{0,6},{2,4},{4,2},{6,0},{1,7},{3,5},{5,3},{7,1},{8,14},{10,12},{12... | collective-permute-start | bytes 995336 | tf_op jit(solution)/shard_map/ppermute | solution.py:339
  (93 other events, 420.7 us)

commit v2 on v1

--- a/solution.py
+++ b/solution.py
@@ -31,12 +31,26 @@
     return cdf, pdf
 
 
+def row_scale(value):
+    return lax.rsqrt(jnp.mean(value * value, axis=-1, keepdims=True) + EPSILON)
+
+
+def mini_scale():
+    row = lax.broadcasted_iota(jnp.int32, (MINI, MINI), 0)
+    col = lax.broadcasted_iota(jnp.int32, (MINI, MINI), 1)
+    return row, col, jnp.where(col <= row, 1.0 / (row + 1).astype(F32), 0.0)
+
+
 def fwd_kernel(
-    kq_ref, kmv_ref, qf_ref, aux_ref, w1i_ref, c1i_ref, w2i_ref, c2i_ref,
-    mixed_ref, w1s_ref, w2s_ref, h_ref, r_ref, g1_ref, g2_ref, ga_ref, ug_ref, gp_ref,
-    w1_ref, c1_ref, w2_ref, c2_ref, *, unroll,
+    length_ref, x_ref, gain_ref, wc_ref, lr_ref, lrt_ref, w1i_ref, c1i_ref, w2i_ref, c2i_ref, pg_ref, pb_ref,
+    post_ref, kq_ref, mix_ref, rate_ref, fac_ref, gl_ref, gs_ref, unit_ref, hscale_ref,
+    w1s_ref, w2s_ref, h_ref, r_ref, g1_ref, g2_ref, ga_ref, ug_ref, gp_ref,
+    w1_ref, c1_ref, w2_ref, c2_ref, kmv_ref, qf_ref, s1_ref, mixed_ref, *, first, unroll,
 ):
     chains, group = kq_ref.shape[:2]
+    rows = group * MINI
+    head_dim = kq_ref.shape[-1]
+    cols = chains * head_dim
 
     @pl.when(pl.program_id(0) == 0)
     def _():
@@ -45,15 +59,44 @@
         w2_ref[...] = w2i_ref[...]
         c2_ref[...] = c2i_ref[...]
 
+    start = (first + pl.program_id(0)) * rows
+    x = x_ref[...].astype(F32)
+    normed = (x * row_scale(x) * gain_ref[...]).astype(BF)
+    proj = mm(normed, wc_ref[...])
+    length = length_ref[0]
+    live_col = start + lax.broadcasted_iota(jnp.int32, (rows, 128), 0) < length
+    live_row = start + lax.broadcasted_iota(jnp.int32, (lrt_ref.shape[0], rows), 1) < length
+    eta_col = jnp.where(live_col, jax.nn.sigmoid(mm(normed, lr_ref[...])), 0.0) * (ETA_BASE / head_dim)
+    rate = jax.nn.sigmoid(mm_nt(lrt_ref[...], normed))
+    eta_row = jnp.where(live_row, rate, 0.0) * (ETA_BASE / head_dim)
+    fac_ref[0] = eta_row * (1.0 - rate)
+    scale = mini_scale()[2]
+    for i in range(chains):
+        at = i * head_dim
+        q = proj[:, at : at + head_dim]
+        k = proj[:, cols + at : cols + at + head_dim]
+        v = proj[:, 2 * cols + at : 2 * cols + at + head_dim]
+        kb, qb = k.astype(BF), q.astype(BF)
+        kq_ref[i, :, :MINI] = kb.reshape(group, MINI, head_dim)
+        kq_ref[i, :, MINI:] = qb.reshape(group, MINI, head_dim)
+        kmv_ref[i] = (k - v).reshape(group, MINI, head_dim)
+        qf_ref[i] = q.reshape(group, MINI, head_dim)
+        rate_ref[i] = (eta_col[:, i : i + 1] * (1.0 / MINI)).reshape(group, MINI, 1)
+        cross = mm_nt(qb, kb) + 1.0
+        for j in range(group):
+            piece = slice(j * MINI, j * MINI + MINI)
+            mix = scale * eta_row[i : i + 1, piece]
+            mix_ref[i, j] = mix
+            s1_ref[i, j] = (mix * cross[piece, piece]).astype(BF)
+
     every = range(chains)
 
     def step(j):
         kq = [kq_ref[i, j] for i in every]
         k = [kq[i][:MINI] for i in every]
-        q = [kq[i][MINI:] for i in every]
-        aux = [aux_ref[i, j] for i in every]
-        mix = [aux[i][:, :MINI] for i in every]
-        rate = [aux[i][:, MINI : MINI + 1] for i in every]
+        mix = [mix_ref[i, j] for i in every]
+        rate = [rate_ref[i, j] for i in every]
+        s1 = [s1_ref[i, j] for i in every]
         kmv = [kmv_ref[i, j] for i in every]
         qf = [qf_ref[i, j] for i in every]
         w1 = [w1_ref[i] for i in every]
@@ -63,7 +106,6 @@
         w1b = [w1[i].astype(BF) for i in every]
         w2b = [w2[i].astype(BF) for i in every]
         both = [mm(kq[i], w1b[i]) + c1[i] for i in every]
-        qk = [mm_nt(q[i], k[i]) for i in every]
         parts = [gelu_parts(both[i][:MINI]) for i in every]
         slope = [parts[i][0] + both[i][:MINI] * parts[i][1] for i in every]
         hb = [(both[i][:MINI] * parts[i][0]).astype(BF) for i in every]
@@ -79,7 +121,6 @@
         c1n = [c1[i] - jnp.sum(fg1[i], axis=0, keepdims=True) for i in every]
         g1b = [g1[i].astype(BF) for i in every]
         ug = [u[i] * (parts[i][1] * (2.0 - both[i][:MINI] * both[i][:MINI])) for i in every]
-        s1 = [(mix[i] * (qk[i] + 1.0)).astype(BF) for i in every]
         pre = [both[i][MINI:] - mm(s1[i], g1b[i]) for i in every]
         parts_q = [gelu_parts(pre[i]) for i in every]
         gp = [parts_q[i][0] + pre[i] * parts_q[i][1] for i in every]
@@ -109,25 +150,64 @@
 
     lax.fori_loop(0, group // unroll, body, 0)
 
+    for i in range(chains):
+        at = i * head_dim
+        gate = proj[:, 3 * cols + at : 3 * cols + at + head_dim]
+        mixed = mixed_ref[i].reshape(rows, head_dim)
+        centered = mixed - jnp.mean(mixed, axis=-1, keepdims=True)
+        hscale = row_scale(centered)
+        unit = centered * hscale
+        out = unit * pg_ref[i] + pb_ref[i]
+        cdf, pdf = gelu_parts(gate)
+        post_ref[:, at : at + head_dim] = (gate * cdf * out).astype(BF)
+        gl_ref[i] = gate * cdf
+        gs_ref[i] = (cdf + gate * pdf) * out
+        unit_ref[i] = unit
+        hscale_ref[i] = hscale
+
 
 def bwd_kernel(
-    d_ref, kq_ref, aux_ref, w1s_ref, w2s_ref, h_ref, r_ref, g1_ref, g2_ref, ga_ref, ug_ref, gp_ref,
-    dq_ref, dk_ref, dv_ref, de_ref, dw1_ref, dc1_ref, dw2_ref, dc2_ref,
-    *, unroll,
+    x_ref, gain_ref, wc_ref, lrt_ref, pg_ref, gpost_ref, w1i_ref, c1i_ref, w2i_ref, c2i_ref,
+    kq_ref, mix_ref, rate_ref, fac_ref, gl_ref, gs_ref, unit_ref, hscale_ref,
+    w1s_ref, w2s_ref, h_ref, r_ref, g1_ref, g2_ref, ga_ref, ug_ref, gp_ref,
+    back_ref, gw_ref, glr_ref, gain_grad_ref, gpg_ref, gpb_ref, dw1_ref, dc1_ref, dw2_ref, dc2_ref,
+    d_ref, dq_ref, dk_ref, dv_ref, de_ref, all_ref, *, unroll,
 ):
     chains, group = kq_ref.shape[:2]
+    rows = group * MINI
+    head_dim = kq_ref.shape[-1]
+    cols = chains * head_dim
 
     @pl.when(pl.program_id(0) == 0)
     def _():
-        dw1_ref[...] = jnp.zeros_like(dw1_ref)
-        dc1_ref[...] = jnp.zeros_like(dc1_ref)
-        dw2_ref[...] = jnp.zeros_like(dw2_ref)
-        dc2_ref[...] = jnp.zeros_like(dc2_ref)
-
-    row = lax.broadcasted_iota(jnp.int32, (MINI, MINI), 0)
-    col = lax.broadcasted_iota(jnp.int32, (MINI, MINI), 1)
-    scale = jnp.where(col <= row, 1.0 / (row + 1).astype(F32), 0.0)
+        dw1_ref[...] = w1i_ref[...]
+        dc1_ref[...] = c1i_ref[...]
+        dw2_ref[...] = w2i_ref[...]
+        dc2_ref[...] = c2i_ref[...]
+        gw_ref[...] = jnp.zeros_like(gw_ref)
+        glr_ref[...] = jnp.zeros_like(glr_ref)
+        gain_grad_ref[...] = jnp.zeros_like(gain_grad_ref)
+        gpg_ref[...] = jnp.zeros_like(gpg_ref)
+        gpb_ref[...] = jnp.zeros_like(gpb_ref)
+
+    row, col, scale = mini_scale()
     eye = jnp.where(col == row, 1.0 / MINI, 0.0)
+    gpost = gpost_ref[...].astype(F32)
+    for i in range(chains):
+        at = i * head_dim
+        piece = gpost[:, at : at + head_dim]
+        all_ref[:, 3 * cols + at : 3 * cols + at + head_dim] = (piece * gs_ref[i]).astype(BF)
+        head = piece * gl_ref[i]
+        unit = unit_ref[i]
+        gpg_ref[i] += jnp.sum(head * unit, axis=0, keepdims=True)
+        gpb_ref[i] += jnp.sum(head, axis=0, keepdims=True)
+        lifted = head * pg_ref[i]
+        grad = hscale_ref[i] * (
+            lifted
+            - jnp.mean(lifted, axis=-1, keepdims=True)
+            - unit * jnp.mean(lifted * unit, axis=-1, keepdims=True)
+        )
+        d_ref[i] = grad.reshape(group, MINI, head_dim)
 
     every = range(chains)
 
@@ -135,7 +215,7 @@
         def all_of(ref):
             return [ref[i, j] for i in every]
 
-        d, kq, aux = all_of(d_ref), all_of(kq_ref), all_of(aux_ref)
+        d, kq = all_of(d_ref), all_of(kq_ref)
         w1b, w2b, hb, rb, g1b, g2b = (
             all_of(ref) for ref in (w1s_ref, w2s_ref, h_ref, r_ref, g1_ref, g2_ref)
         )
@@ -146,8 +226,7 @@
         dc2 = [dc2_ref[i] for i in every]
         k = [kq[i][:MINI] for i in every]
         q = [kq[i][MINI:] for i in every]
-        mix = [aux[i][:, :MINI] for i in every]
-        rate = [aux[i][:, MINI : MINI + 1] for i in every]
+        mix, rate = all_of(mix_ref), all_of(rate_ref)
         g1 = [g1b[i].astype(F32) for i in every]
         g2 = [g2b[i].astype(F32) for i in every]
         dw1b = [dw1[i].astype(BF) for i in every]
@@ -224,80 +303,139 @@
 
     lax.fori_loop(0, group // unroll, body, 0)
 
-
-def run_fwd(kq, kmv, qf, aux, w1, c1, w2, c2, group=8, unroll=2):
-    chains, count, _, hd = kq.shape
-    inner = w1.shape[-1]
-    steps = count // group
-
-    def spec(rows, cols):
-        return pl.BlockSpec((chains, group, rows, cols), lambda g: (0, g, 0, 0))
-
-    def whole(rows, cols):
-        return pl.BlockSpec((chains, rows, cols), lambda g: (0, 0, 0))
-
-    def out(rows, cols, dtype):
-        return jax.ShapeDtypeStruct((chains, count, rows, cols), dtype)
-
+    x = x_ref[...].astype(F32)
+    unit_in = x * row_scale(x)
+    normed = (unit_in * gain_ref[...]).astype(BF)
+    lrt = lrt_ref[...]
+    padded = lrt.shape[0]
+    which = lax.broadcasted_iota(jnp.int32, (padded, rows), 0)
+    rates = jnp.zeros((padded, rows), F32)
+    for i in range(chains):
+        at = i * head_dim
+        all_ref[:, at : at + head_dim] = dq_ref[i].reshape(rows, head_dim)
+        all_ref[:, cols + at : cols + at + head_dim] = dk_ref[i].reshape(rows, head_dim)
+        all_ref[:, 2 * cols + at : 2 * cols + at + head_dim] = dv_ref[i].reshape(rows, head_dim)
+        line = jnp.concatenate([de_ref[i, j] for j in range(group)], axis=1)
+        rates = jnp.where(which == i, line, rates)
+    rates = (rates * fac_ref[0]).astype(BF)
+    grads = all_ref[...]
+    back = mm_nt(grads, wc_ref[...]) + mm_tn(rates, lrt)
+    gain_grad_ref[...] += jnp.sum(back * unit_in, axis=0, keepdims=True)
+    back_ref[...] = back.astype(BF)
+    gw_ref[...] += mm_tn(normed, grads)
+    glr_ref[...] += mm(rates, normed)
+
+
+GROUP = 8
+
+
+def block_specs(chains, head_dim, inner, padded, place):
+    rows = GROUP * MINI
+
+    def mini(first, second):
+        return pl.BlockSpec((chains, GROUP, first, second), lambda g: (0, place(g), 0, 0))
+
+    def head(second):
+        return pl.BlockSpec((chains, rows, second), lambda g: (0, place(g), 0))
+
+    return [
+        mini(2 * MINI, head_dim), mini(MINI, MINI), mini(MINI, 1),
+        pl.BlockSpec((1, padded, rows), lambda g: (place(g), 0, 0)),
+        head(head_dim), head(head_dim), head(head_dim), head(1),
+        mini(head_dim, inner), mini(head_dim, inner), mini(MINI, inner), mini(MINI, inner),
+        mini(MINI, inner), mini(MINI, head_dim), mini(MINI, inner), mini(MINI, inner), mini(MINI, inner),
+    ]
+
+
+def whole_spec(value):
+    return pl.BlockSpec(value.shape, lambda g: (0,) * value.ndim)
+
+
+def run_fwd(first, last, length, tokens, gain, wc, lr, lrt, pg, pb, state, unroll=2):
+    width = tokens.shape[1]
+    chains, head_dim, inner = state[0].shape
+    rows = GROUP * MINI
+    steps = last - first
+    count = steps * GROUP
+    padded = lrt.shape[0]
+
+    def mini(first_size, second_size, dtype):
+        return jax.ShapeDtypeStruct((chains, count, first_size, second_size), dtype)
+
+    def head(second):
+        return jax.ShapeDtypeStruct((chains, steps * rows, second), F32)
+
+    row_spec = pl.BlockSpec((rows, width), lambda g: (first + g, 0))
+    small = (gain, wc, lr, lrt, *state, pg, pb)
     return pl.pallas_call(
-        partial(fwd_kernel, unroll=unroll),
+        partial(fwd_kernel, first=first, unroll=unroll),
         grid=(steps,),
-        in_specs=[spec(2 * MINI, hd), spec(MINI, hd), spec(MINI, hd), spec(MINI, 128),
-                  whole(hd, inner), whole(1, inner), whole(hd, inner), whole(1, hd)],
-        out_specs=[spec(MINI, hd), spec(hd, inner), spec(hd, inner), spec(MINI, inner), spec(MINI, inner),
-                   spec(MINI, inner), spec(MINI, hd), spec(MINI, inner), spec(MINI, inner), spec(MINI, inner)],
-        out_shape=[out(MINI, hd, F32), out(hd, inner, BF), out(hd, inner, BF), out(MINI, inner, BF), out(MINI, inner, BF),
-                   out(MINI, inner, BF), out(MINI, hd, BF), out(MINI, inner, F32), out(MINI, inner, F32), out(MINI, inner, F32)],
-        scratch_shapes=[pltpu.VMEM((chains, hd, inner), F32), pltpu.VMEM((chains, 1, inner), F32),
-                        pltpu.VMEM((chains, hd, inner), F32), pltpu.VMEM((chains, 1, hd), F32)],
-        compiler_params=pltpu.CompilerParams(vmem_limit_bytes=48 << 20),
-        cost_estimate=pl.CostEstimate(flops=60_000_000_000, bytes_accessed=40_000_000, transcendentals=0),
+        in_specs=[pl.BlockSpec(memory_space=pltpu.SMEM), row_spec] + [whole_spec(v) for v in small],
+        out_specs=[pl.BlockSpec((rows, chains * head_dim), lambda g: (g, 0))]
+        + block_specs(chains, head_dim, inner, padded, lambda g: g)
+        + [whole_spec(v) for v in state],
+        out_shape=[
+            jax.ShapeDtypeStruct((steps * rows, chains * head_dim), BF),
+            mini(2 * MINI, head_dim, BF), mini(MINI, MINI, F32), mini(MINI, 1, F32),
+            jax.ShapeDtypeStruct((steps, padded, rows), F32),
+            head(head_dim), head(head_dim), head(head_dim), head(1),
+            mini(head_dim, inner, BF), mini(head_dim, inner, BF), mini(MINI, inner, BF), mini(MINI, inner, BF),
+            mini(MINI, inner, BF), mini(MINI, head_dim, BF), mini(MINI, inner, F32), mini(MINI, inner, F32),
+            mini(MINI, inner, F32),
+        ]
+        + [jax.ShapeDtypeStruct(v.shape, F32) for v in state],
+        scratch_shapes=[
+            pltpu.VMEM((chains, GROUP, MINI, head_dim), F32), pltpu.VMEM((chains, GROUP, MINI, head_dim), F32),
+            pltpu.VMEM((chains, GROUP, MINI, MINI), BF), pltpu.VMEM((chains, GROUP, MINI, head_dim), F32),
+        ],
+        compiler_params=pltpu.CompilerParams(vmem_limit_bytes=50 << 20),
+        cost_estimate=pl.CostEstimate(
+            flops=9_000_000_000 * steps, bytes_accessed=5_000_000 * steps, transcendentals=0
+        ),
         name="chain_forward",
-    )(kq, kmv, qf, aux, w1, c1, w2, c2)
-
-
-def run_bwd(d, kq, aux, saved, group=8, unroll=2):
-    chains, count, _, hd = kq.shape
-    inner = saved[0].shape[-1]
-    steps = count // group
-
-    def spec(rows, cols):
-        return pl.BlockSpec((chains, group, rows, cols), lambda g: (0, steps - 1 - g, 0, 0))
-
-    def whole(rows, cols):
-        return pl.BlockSpec((chains, rows, cols), lambda g: (0, 0, 0))
-
-    def out(rows, cols, dtype):
-        return jax.ShapeDtypeStruct((chains, count, rows, cols), dtype)
-
-    def st(rows, cols):
-        return jax.ShapeDtypeStruct((chains, rows, cols), F32)
-
+    )(length, tokens, *small)
+
+
+def run_bwd(first, last, tokens, gain, wc, lrt, pg, gpost, state, saved, unroll=2):
+    width = tokens.shape[1]
+    chains, head_dim, inner = state[0].shape
+    rows = GROUP * MINI
+    padded = lrt.shape[0]
+    wide = wc.shape[1]
+    steps = last - first
+
+    def place(g):
+        return steps - 1 - g
+
+    def shape(*extent):
+        return jax.ShapeDtypeStruct(extent, F32)
+
+    small = (gain, wc, lrt, pg)
+    outs = [
+        shape(width, wide), shape(padded, width), shape(1, width), shape(chains, 1, head_dim), shape(chains, 1, head_dim),
+        shape(chains, head_dim, inner), shape(chains, 1, inner), shape(chains, head_dim, inner), shape(chains, 1, head_dim),
+    ]
+    scratch = pltpu.VMEM((chains, GROUP, MINI, head_dim), BF)
     return pl.pallas_call(
         partial(bwd_kernel, unroll=unroll),
         grid=(steps,),
-        in_specs=[spec(MINI, hd), spec(2 * MINI, hd), spec(MINI, 128), spec(hd, inner), spec(hd, inner),
-                  spec(MINI, inner), spec(MINI, inner), spec(MINI, inner), spec(MINI, hd),
-                  spec(MINI, inner), spec(MINI, inner), spec(MINI, inner)],
-        out_specs=[spec(MINI, hd), spec(MINI, hd), spec(MINI, hd), spec(1, MINI),
-                   whole(hd, inner), whole(1, inner), whole(hd, inner), whole(1, hd)],
-        out_shape=[out(MINI, hd, BF), out(MINI, hd, BF), out(MINI, hd, BF), out(1, MINI, F32),
-                   st(hd, inner), st(1, inner), st(hd, inner), st(1, hd)],
-        compiler_params=pltpu.CompilerParams(vmem_limit_bytes=48 << 20),
-        cost_estimate=pl.CostEstimate(flops=70_000_000_000, bytes_accessed=40_000_000, transcendentals=0),
+        in_specs=[pl.BlockSpec((rows, width), lambda g: (first + place(g), 0))]
+        + [whole_spec(v) for v in small]
+        + [pl.BlockSpec((rows, chains * head_dim), lambda g: (first + place(g), 0))]
+        + [whole_spec(v) for v in state]
+        + block_specs(chains, head_dim, inner, padded, place),
+        out_specs=[pl.BlockSpec((rows, width), lambda g: (place(g), 0))] + [whole_spec(v) for v in outs],
+        out_shape=[jax.ShapeDtypeStruct((steps * rows, width), BF)] + outs,
+        scratch_shapes=[
+            pltpu.VMEM((chains, GROUP, MINI, head_dim), F32), scratch, scratch, scratch,
+            pltpu.VMEM((chains, GROUP, 1, MINI), F32), pltpu.VMEM((rows, wide), BF),
+        ],
+        compiler_params=pltpu.CompilerParams(vmem_limit_bytes=50 << 20),
+        cost_estimate=pl.CostEstimate(
+            flops=11_000_000_000 * steps, bytes_accessed=5_000_000 * steps, transcendentals=0
+        ),
         name="chain_backward",
-    )(d, kq, aux, *saved)
-
-
-def gelu(value):
-    return jax.nn.gelu(value, approximate=False)
-
-
-def gelu_slope(value):
-    return (
-        0.5 * (1.0 + lax.erf(value * 0.7071067811865476))
-        + value * jnp.exp(-0.5 * value * value) * 0.3989422804014327
-    )
+    )(tokens, *small, gpost, *state, *saved)
 
 
 def row_norm(value):
@@ -329,16 +467,49 @@
     return lax.ppermute(value, "tp", [(0, 1), (1, 0)])
 
 
+def place_kernel(spots_ref, *refs):
+    *sources, target, sems = refs
+    copies = [
+        pltpu.make_async_copy(source, target.at[spots_ref[number]], sems.at[number])
+        for number, source in enumerate(sources)
+    ]
+    for copy in copies:
+        copy.start()
+    for copy in copies:
+        copy.wait()
+
+
+def placed(pieces, spots):
+    anywhere = pl.BlockSpec(memory_space=pl.ANY)
+    return pl.pallas_call(
+        place_kernel,
+        in_specs=[pl.BlockSpec(memory_space=pltpu.SMEM)] + [anywhere] * len(pieces),
+        out_specs=anywhere,
+        out_shape=jax.ShapeDtypeStruct((len(pieces),) + pieces[0].shape, pieces[0].dtype),
+        scratch_shapes=[pltpu.SemaphoreType.DMA((len(pieces),))],
+        name="place_pieces",
+    )(jnp.stack(spots).astype(jnp.int32), *pieces)
+
+
+def exchanged(value, axis):
+    size = lax.axis_size(axis)
+    return [value] + [
+        lax.ppermute(value, axis, [(source, source ^ bit) for source in range(size)])
+        for bit in range(1, size)
+    ]
+
+
+def placed_along(pieces, axis):
+    me = lax.axis_index(axis)
+    return placed(pieces, [me ^ bit for bit in range(len(pieces))])
+
+
 def spread(value, axis):
-    size = lax.axis_size(axis)
-    me = lax.axis_index(axis)
-    whole = lax.dynamic_update_index_in_dim(
-        jnp.zeros((size,) + value.shape, value.dtype), value, me, 0
-    )
-    for bit in range(1, size):
-        piece = lax.ppermute(value, axis, [(source, source ^ bit) for source in range(size)])
-        whole = lax.dynamic_update_index_in_dim(whole, piece, me ^ bit, 0)
-    return whole
+    return placed_along(exchanged(value, axis), axis)
+
+
+def tied(*values):
+    return lax.optimization_barrier(values)
 
 
 def in_turn(first, second):
@@ -395,7 +566,7 @@
     pieces = pieces_of(chains, depth, head_dim, inner_share, head_share)
     small_size = sum(size_of(shape) for _, shape in pieces)
     small_rows = -(-small_size // wide)
-    small_rows = -(-(small_rows + depth) // 16) * 16 - depth
+    small_rows = -(-(small_rows + depth) // 32) * 32 - depth
     half_rows = (small_rows + depth) // 2
     own = {
         "lr": of_heads(lr_weight, 1),
@@ -425,8 +596,8 @@
     row_pack = jnp.concatenate([ffn_gate, ffn_up, ffn_down.T, out_weight.T], axis=1)
     part = depth // ring
     row_part = lax.dynamic_slice_in_dim(row_pack, place * part, part, 0)
-    row_part, gathered = lax.optimization_barrier((row_part, gathered))
-    row_part = spread(row_part, "shard")
+    row_part, gathered = tied(row_part, gathered)
+    row_parts = exchanged(row_part, "shard")
 
     w_chain = gathered[:, :depth].reshape(width, wide)
     flat = gathered[:, depth:].reshape(shards, small_rows * wide)
@@ -446,60 +617,45 @@
     init_first_bias, init_second_bias = along("b1"), along("b2")
     norm_gain, norm_bias = along("pg"), along("pb")
 
-    slot_length = lax.dynamic_index_in_dim(lengths, core, 0, keepdims=False)
-    live_all = (lax.iota(jnp.int32, span_all) < slot_length).astype(F32)
-    slot_in = slot_tokens.astype(F32)
-    unit_in = slot_in * row_norm(slot_in)
-    normed_one = (unit_in * gain_one).astype(BF)
-    projected = mm(normed_one, w_chain).reshape(span_all, 4, chains, head_dim).transpose(1, 2, 0, 3)
-    queries, keys, values, gate_pre = (projected[i] for i in range(4))
-    gate_rate = jax.nn.sigmoid(mm(normed_one, w_rate))
-    eta = ETA_BASE / head_dim * gate_rate * live_all[:, None]
-    eta_blocks = eta.T.reshape(chains, count, MINI)
-
-    def blocks(value):
-        return value.reshape(chains, count, MINI, value.shape[-1])
-
-    row_index = lax.broadcasted_iota(jnp.int32, (MINI, MINI), 0)
-    col_index = lax.broadcasted_iota(jnp.int32, (MINI, MINI), 1)
-    scale = jnp.where(col_index <= row_index, 1.0 / (row_index + 1).astype(F32), 0.0)
-    aux = jnp.concatenate(
-        [
-            scale * eta_blocks[:, :, None, :],
-            eta_blocks[..., None] / MINI,
-            jnp.zeros((chains, count, MINI, 128 - MINI - 1), F32),
-        ],
-        axis=-1,
-    )
-    kq = jnp.concatenate([blocks(keys), blocks(queries)], axis=2).astype(BF)
-    kq, row_part = lax.optimization_barrier((kq, row_part))
-    row_all = spread(row_part, "ctx")
-    forward = run_fwd(
-        kq,
-        blocks(keys - values),
-        blocks(queries),
-        aux,
-        init_first,
-        init_first_bias[:, None],
-        init_second,
-        init_second_bias[:, None],
-    )
-    mixed, saved = forward[0].reshape(chains, span_all, head_dim), forward[1:]
-
-    centered = mixed - jnp.mean(mixed, axis=-1, keepdims=True)
-    scale_head = lax.rsqrt(jnp.mean(centered * centered, axis=-1, keepdims=True) + EPSILON)
-    unit = centered * scale_head
-    head_out = unit * norm_gain[:, None] + norm_bias[:, None]
-    post_chain = (gelu(gate_pre) * head_out).astype(BF)
+    slot_length = lax.dynamic_index_in_dim(lengths, core, 0, keepdims=True)
+    gain_row = gain_one[None]
+    rate_cols = jnp.pad(w_rate, ((0, 0), (0, 128 - chains)))
+    rate_rows = jnp.pad(w_rate.T, ((0, -chains % 16), (0, 0)))
+    norm_gain, norm_bias = norm_gain[:, None], norm_bias[:, None]
+    steps = span_all // (GROUP * MINI)
+    middle = steps // 2
+    state = (init_first, init_first_bias[:, None], init_second, init_second_bias[:, None])
+
+    def forward(first, last, begin):
+        done = run_fwd(
+            first, last, slot_length, slot_tokens, gain_row, w_chain, rate_cols, rate_rows, norm_gain, norm_bias, begin
+        )
+        return done[0], done[1:-4], done[-4:]
+
+    post_low, saved_low, state_low = forward(0, middle, state)
+    state_low, row_parts = tied(state_low, row_parts)
+    far = jnp.stack(row_parts[1:])
+    state_low, far = tied(state_low, far)
+    far_parts = exchanged(far, "ctx")
+    post_high, saved_high, _ = forward(middle, steps, tuple(state_low))
+    post_chain = jnp.concatenate([post_low, post_high])
 
     def to_rows(value):
         return lax.all_to_all(value.reshape(ring, span, -1), "ctx", 0, 0)
 
-    post = to_rows(post_chain.transpose(1, 0, 2).reshape(span_all, cols))
+    post = to_rows(post_chain)
     post = post.transpose(1, 0, 2).reshape(span, ring * cols)[:, : total_heads * head_dim]
 
-    w_own = row_all.transpose(1, 0, 2, 3).reshape(width, -1)
-    w_other = swap(w_own)
+    far_parts, post = tied(far_parts, post)
+    me = lax.axis_index("shard")
+    blocks = [row_pack[start : start + part] for start in range(0, depth, part)]
+    spots = [me * ring + number for number in range(ring)]
+    for bit, group in enumerate(far_parts):
+        for other in range(1, shards):
+            blocks.append(group[other - 1])
+            spots.append((me ^ other) * ring + (place ^ bit))
+    w_own = placed(blocks, spots).reshape(width, -1)
+    w_other = jnp.concatenate([swap(w_own[:, : 3 * units]), swap(w_own[:, 3 * units :])], axis=1)
 
     def split_up(value):
         return tuple(value[:, start : start + units] for start in range(0, 3 * units, units))
@@ -517,7 +673,7 @@
     scale_two = row_norm(hidden)
     normed_two = (hidden * scale_two * gain_two).astype(BF)
     position = place * span + lax.iota(jnp.int32, span)
-    live = (position < slot_length).astype(F32)[:, None]
+    live = (position < slot_length[0]).astype(F32)[:, None]
     cot = lax.dynamic_index_in_dim(cotangent, core, 0, keepdims=False)
     back = cot.astype(F32) * live
     back_low = back.astype(BF)
@@ -558,34 +714,40 @@
     own_sum = jnp.concatenate(sums[0] + [grad_out_own], axis=1)
     other_sum = jnp.concatenate(sums[1] + [grad_out_other], axis=1).astype(BF)
     row_sum = (own_sum + swap(other_sum).astype(F32)).astype(BF)
-    row_sum = lax.all_to_all(row_sum.reshape(shards * ring, part, -1), ("shard", "ctx"), 0, 0)
+    row_sum = row_sum.reshape(shards, ring, part, -1).transpose(1, 0, 2, 3)
+    cut = 2 * units
+    sum_a = lax.all_to_all(row_sum[..., :cut], "ctx", 0, 0)
+    sum_b = lax.all_to_all(row_sum[..., cut:], "ctx", 0, 0)
+
+    def folded(value):
+        return jnp.sum(value.astype(F32), axis=0).astype(BF)
 
     grad_post = jnp.pad(grad_post.astype(BF), ((0, 0), (0, ring * cols - total_heads * head_dim)))
     grad_post = lax.all_to_all(grad_post.reshape(span, ring, cols).transpose(1, 0, 2), "ctx", 0, 0)
-    grad_post = grad_post.reshape(span_all, chains, head_dim).transpose(1, 0, 2).astype(F32)
-    grad_gate_pre = (grad_post * gelu_slope(gate_pre) * head_out).astype(BF)
-    grad_head = grad_post * gelu(gate_pre)
-    grad_norm_gain = jnp.sum(grad_head * unit, axis=1)
-    grad_norm_bias = jnp.sum(grad_head, axis=1)
-    lifted = grad_head * norm_gain[:, None]
-    grad_mixed = scale_head * (
-        lifted
-        - jnp.mean(lifted, axis=-1, keepdims=True)
-        - unit * jnp.mean(lifted * unit, axis=-1, keepdims=True)
-    )
-    grad_q, grad_k, grad_v, grad_eta, d_first, d_first_bias, d_second, d_second_bias = run_bwd(
-        blocks(grad_mixed), kq, aux, saved
-    )
-    grad_eta = grad_eta.reshape(chains, span_all).T
-    grad_rate = grad_eta * (ETA_BASE / head_dim) * gate_rate * (1.0 - gate_rate) * live_all[:, None]
-    grad_rate_low = grad_rate.astype(BF)
-    grad_all = jnp.stack(
-        [value.reshape(chains, span_all, head_dim) for value in (grad_q, grad_k, grad_v, grad_gate_pre)]
-    )
-    grad_all = grad_all.transpose(2, 0, 1, 3).reshape(span_all, wide)
-    back_part = mm_nt(grad_all, w_chain) + mm_nt(grad_rate_low, w_rate)
-    grad_gain_one = jnp.sum(back_part * unit_in, axis=0)
-    back_one = jnp.sum(to_rows(back_part.astype(BF)).astype(F32), axis=0)
+    grad_post = grad_post.reshape(span_all, cols)
+
+    def backward(first, last, begin, saved):
+        done = run_bwd(
+            first, last, slot_tokens, gain_row, w_chain, rate_rows, norm_gain, grad_post, begin, saved
+        )
+        return done[0], done[1:6], done[6:]
+
+    begin = tuple(jnp.zeros_like(value) for value in state)
+    grad_post, row_sum = tied(grad_post, row_sum)
+    back_high, sums_high, ending = backward(middle, steps, begin, saved_high)
+    ending, sum_a = tied(ending, sum_a)
+    sum_a = folded(sum_a)
+    ending, sum_a = tied(ending, sum_a)
+    sum_a = lax.all_to_all(sum_a, "shard", 0, 0)
+    back_low_half, sums_low, ending = backward(0, middle, tuple(ending), saved_low)
+    ending, back_low_half, sum_a, sum_b = tied(ending, back_low_half, sum_a, sum_b)
+    d_first, d_first_bias, d_second, d_second_bias = ending
+    grad_big, grad_lr, grad_gain_one, grad_norm_gain, grad_norm_bias = (
+        low + high for low, high in zip(sums_low, sums_high)
+    )
+    grad_lr = grad_lr[:chains].T
+    back_part = jnp.concatenate([back_low_half, back_high])
+    back_one = jnp.sum(to_rows(back_part).astype(F32), axis=0)
     scale_one = row_norm(row_in)
     lifted = back_one * gain_one
     input_grad = (
@@ -594,15 +756,14 @@
         - row_in * scale_one**3 * jnp.mean(lifted * row_in, axis=-1, keepdims=True)
     ).astype(BF)
 
-    row_sum = spread(jnp.sum(row_sum.astype(F32), axis=0).astype(BF), "ctx")
+    sum_b = lax.all_to_all(folded(sum_b), "shard", 0, 0)
+    row_sum = spread(jnp.concatenate([folded(sum_a), folded(sum_b)], axis=-1), "ctx")
     row_sum = row_sum.reshape(depth, -1).astype(F32)
     g_ffn_gate = row_sum[:, :units]
     g_ffn_up = row_sum[:, units : 2 * units]
     g_ffn_down = row_sum[:, 2 * units : 3 * units].T
     g_out = row_sum[:, 3 * units :].T
 
-    grad_big = mm_tn(normed_one, grad_all)
-    grad_lr = mm_tn(normed_one, grad_rate_low)
 
     def by_shard(value):
         split = value.reshape(value.shape[:-1] + (shards, -1))
@@ -613,10 +774,10 @@
             grad_lr.reshape(shards, -1),
             by_shard(d_first),
             by_shard(d_second),
-            by_shard(d_first_bias),
-            by_shard(d_second_bias),
-            by_shard(grad_norm_gain),
-            by_shard(grad_norm_bias),
+            by_shard(d_first_bias[:, 0]),
+            by_shard(d_second_bias[:, 0]),
+            by_shard(grad_norm_gain[:, 0]),
+            by_shard(grad_norm_bias[:, 0]),
             grad_gain_one.reshape(shards, -1),
             grad_gain_two.reshape(shards, -1),
         ],

time: 597 us -> 791 us (1.32)
  Pallas kernels: 137 us -> 461 us
  waiting for transfers between devices: 187 us -> 92 us
  local copies, waits for them, and re-layouts: 104 us -> 77.9 us
  matrix products: 53.5 us -> 32.7 us
  starting transfers between devices: 48.4 us -> 65.7 us
  other arithmetic: 56.9 us -> 44.6 us
    pallas_call x1 -> x7, Pallas kernels: 69.1 us -> 372 us  [the longest x5 305 us: placed(): pl.pallas_call(place_kernel, in_specs=[pl.BlockSpec(memory_space=pltpu.SM...]
    ppermute x18, waiting for transfers between devices: 116 us -> 41 us  [exchanged(): lax.ppermute(value, axis, [(source, source ^ bit) for source in range(siz...]
    all_to_all x1 -> x4, waiting for transfers between devices: 60.8 us -> 31.5 us  [the longest x1 29 us: on_device(): sum_a = lax.all_to_all(row_sum[..., :cut], 'ctx', 0, 0)]
    pallas_call x1 -> x2, Pallas kernels: 68.1 us -> 88.8 us  [run_bwd(): pl.pallas_call(partial(bwd_kernel, unroll=unroll), grid=(steps,), in_spec...]
    dynamic_update_slice x24 -> x0, local copies, waits for them, and re-layouts: 17.8 us -> none  [the longest x18 13.4 us: spread(): whole = lax.dynamic_update_index_in_dim(whole, piece, me ^ bit, 0)]
    convert_element_type x18, local copies, waits for them, and re-layouts: 16.9 us -> 2.22 us  [along(): jnp.moveaxis(full[name], 0, -2).reshape(full[name].shape[1:-1] + (-1,))]
    slice x2 -> x5, local copies, waits for them, and re-layouts: 1.64 us -> 15.3 us  [the longest x1 4.95 us: on_device(): w_own[:, :3 * units]]
    all_to_all x1 -> x4, starting transfers between devices: 8.38 us -> 20.2 us  [the longest x1 5.38 us: on_device(): sum_a = lax.all_to_all(sum_a, 'shard', 0, 0)]
  transfers between devices with their start and end apart: 31 -> 35, of which waited for: 13 -> 13; matrix products, arithmetic and copies ran while one was open for 27% -> 10% of each run, Pallas kernels for 23% -> 35%
where the time goes in v2:
time: 791 us; the launch traced here: 776 us
  Pallas kernels  461 us (58%)
  waiting for transfers between devices  92 us (12%)
  local copies, waits for them, and re-layouts  77.9 us (10%)
  starting transfers between devices  65.7 us (8%)
  other arithmetic  44.6 us (6%)
  matrix products  32.7 us (4%)
    pallas_call x5, Pallas kernels, placed(): pl.pallas_call(place_kernel, in_specs=[pl.BlockSpec(memory_space=pltpu.SM...  305 us
    pallas_call x2, Pallas kernels, run_bwd(): pl.pallas_call(partial(bwd_kernel, unroll=unroll), grid=(steps,), in_spec...  88.8 us
    pallas_call x2, Pallas kernels, run_fwd(): pl.pallas_call(partial(fwd_kernel, first=first, unroll=unroll), grid=(ste...  66.6 us
    ppermute x18, waiting for transfers between devices, exchanged(): lax.ppermute(value, axis, [(source, source ^ bit) for source in range(siz...  41 us
    all_to_all x1, waiting for transfers between devices, on_device(): sum_a = lax.all_to_all(row_sum[..., :cut], 'ctx', 0, 0)  29 us
    ppermute x18, starting transfers between devices, exchanged(): lax.ppermute(value, axis, [(source, source ^ bit) for source in range(siz...  21.1 us
    unnamed x133, local copies, waits for them, and re-layouts  19.5 us
  transfers between devices with their start and end apart: 35, of which 13 were waited for; matrix products, arithmetic and copies ran while one was open for 10% of the time, Pallas kernels for 35%

profile of v2, /device:TPU:12, one launch (start us, length us, event | category | flops | bytes accessed | tf_op | source)
XLA Modules:
  0.0 776.0 jit_solution(17559920351955595453)
XLA Ops:
  21.7 7.1 collective-permute-done.5.refs_2_
  32.7 25.6 %place_pieces.6 = bf16[4,128,768]{2,1,0:T(8,128)(2,1)} custom-call(s32[4]{0:T(128)} %pad_add_fusion.1.spots_ref, bf16[128,768]{1,0:T(8,128)(2,1)} %copy-done.44, bf16[128,768]{1,0:T(8,128)(2,1)} %copy-done.59, bf16[128,768]{1,0:T(8,128)(2,1)} %copy-done.60, bf16[128,768]{1,0:T(8,128)(2,1)} %collective-permute-done.6.refs_3_), custom_call_target="tpu_custom_call" | custom-call | tf_op jit(solution)/shard_map/place_pieces/pallas_call | solution.py:484
  61.6 49.4 %place_pieces.5 = bf16[4,256,768]{2,1,0:T(8,128)(2,1)} custom-call(s32[4]{0:T(128)} %pad_add_fusion.spots_ref, bf16[256,768]{1,0:T(8,128)(2,1)} %copy-done.41, bf16[256,768]{1,0:T(8,128)(2,1)} %collective-permute-done.refs_1_, bf16[256,768]{1,0:T(8,128)(2,1)} %collective-permute-done.1.refs_2_, bf16[256,768]{1,0:T(8,128)(2,1)} %copy-done.56), custom_call_target="tpu_custom_call" | custom-call | tf_op jit(solution)/shard_map/place_pieces/pallas_call | solution.py:484
  119.6 33.2 %chain_forward.2 = (bf16[512,192]{1,0:T(8,128)(2,1)S(1)}, bf16[3,32,32,64]{3,2,1,0:T(8,128)(2,1)S(1)}, f32[3,32,16,16]{3,2,1,0:T(8,128)S(1)}, f32[3,32,16,1]{3,2...) custom-call(s32[1]{0:T(128)} %dynamic_slice.60.length_ref, ...), custom_call_target="tpu_custom_call" | custom-call | flops 35999997952 | bytes 20000000 | tf_op jit(solution)/shard_map/chain_forward/pallas_call | solution.py:370
  159.3 33.4 %chain_forward.3 = (bf16[512,192]{1,0:T(8,128)(2,1)S(1)}, bf16[3,32,32,64]{3,2,1,0:T(8,128)(2,1)S(1)}, f32[3,32,16,16]{3,2,1,0:T(8,128)S(1)}, f32[3,32,16,1]{3,2...) custom-call(s32[1]{0:T(128)} %dynamic_slice.60.length_ref, ...), custom_call_target="tpu_custom_call" | custom-call | flops 35999997952 | bytes 20000000 | tf_op jit(solution)/shard_map/chain_forward/pallas_call | solution.py:370
  197.1 5.1 all-to-all-start
  216.4 162.7 %place_pieces.7 = bf16[16,48,3456]{2,1,0:T(8,128)(2,1)} custom-call(s32[16]{0:T(128)} %stack.193.spots_ref, bf16[48,3456]{1,0:T(8,128)(2,1)} %get-tuple-element.231.refs_0_, bf16[48,3456]{1,0:T(8,128)(2,1)} %get-tuple-element.230.refs_1_, bf16[48,3456]{1,0:T(8,128)(2,1)} %get-tuple-element.229.refs_2_, bf16[48,3456]{1,0:T(8,128)(2,1)} %get-tuple-element.228.refs_3_, ...), custom_call_target="tpu_custom_call" | custom-call | tf_op jit(solution)/shard_map/place_pieces/pallas_call | solution.py:484
  379.2 5.0 slice.244
  429.0 4.8 all-to-all-start.1
  433.9 5.9 fusion
  446.7 4.8 all-to-all-start.2
  458.9 29.0 %all-to-all-done.2 = bf16[4,4,48,2048]{3,2,1,0:T(8,128)(2,1)} async-done(((bf16[4,4,48,2048]{3,2,1,0:T(8,128)(2,1)}), bf16[4,4,48,2048]{3,2,1,0:T(8,128)(2,1)}, u32[]{:S(2)}, u32[]{:S(2)}) %all-to-all-start.2) | async-done | bytes 3145760 | tf_op jit(solution)/shard_map/all_to_all | solution.py:719
  487.9 5.0 all-to-all-start.4
  494.1 44.4 %chain_backward.2 = (bf16[512,768]{1,0:T(8,128)(2,1)S(1)}, f32[768,768]{1,0:T(8,128)}, f32[16,768]{1,0:T(8,128)S(1)}, f32[1,768]{1,0:T(1,128)S(1)}, f32[3,1,64]{...) custom-call(bf16[1024,768]{1,0:T(8,128)(2,1)} %bitcast.214, ...), custom_call_target="tpu_custom_call" | custom-call | flops 44000002048 | bytes 20000000 | tf_op jit(solution)/shard_map/chain_backward/pallas_call | solution.py:419
  543.4 5.4 all-to-all-start.3
  551.7 44.4 %chain_backward.3 = (bf16[512,768]{1,0:T(8,128)(2,1)S(1)}, f32[768,768]{1,0:T(8,128)}, f32[16,768]{1,0:T(8,128)S(1)}, f32[1,768]{1,0:T(1,128)S(1)}, f32[3,1,64]{...) custom-call(bf16[1024,768]{1,0:T(8,128)(2,1)} %bitcast.215, ...), custom_call_target="tpu_custom_call" | custom-call | flops 44000002048 | bytes 20000000 | tf_op jit(solution)/shard_map/chain_backward/pallas_call | solution.py:419
  599.9 5.1 all-to-all-start.7
  615.9 4.9 all-to-all-start.5
  632.5 15.4 %collective-permute-done.24.refs_1_ = bf16[48,3456]{1,0:T(8,128)(2,1)S(1)} collective-permute-done((bf16[48,3456]{1,0:T(8,128)(2,1)S(1)}, bf16[48,3456]{1,0:T(8,128)(2,1)S(1)}, u32[]{:S(2)}, u32[]{:S(2)}) %collective-permute-start.24) | collective-permute-done | bytes 331808 | tf_op jit(solution)/shard_map/ppermute | solution.py:497
  648.0 4.7 collective-permute-done.26.refs_3_
  652.7 42.0 %place_pieces.9 = bf16[4,48,3456]{2,1,0:T(8,128)(2,1)} custom-call(s32[4]{0:T(128)} %pad_add_fusion.spots_ref, bf16[48,3456]{1,0:T(8,128)(2,1)} %copy-done.43, bf16[48,3456]{1,0:T(8,128)(2,1)} %copy-done.57, bf16[48,3456]{1,0:T(8,128)(2,1)} %copy-done.58, bf16[48,3456]{1,0:T(8,128)(2,1)} %collective-permute-done.26.refs_3_), custom_call_target="tpu_custom_call" | custom-call | tf_op jit(solution)/shard_map/place_pieces/pallas_call | solution.py:484
  694.8 8.0 %all-to-all-start.6 = ((bf16[4,128,768]{2,1,0:T(8,128)(2,1)}), bf16[4,128,768]{2,1,0:T(8,128)(2,1)}, u32[]{:S(2)}, u32[]{:S(2)}) async-start(bf16[4,128,768]{2,1,0:T(8,128)(2,1)} %add_convert_fusion.1), calls=%async_computation.6 | async-start | bytes 1572864 | tf_op jit(solution)/shard_map/all_to_all | solution.py:793
  707.2 11.0 %all-to-all-done.6 = bf16[4,128,768]{2,1,0:T(8,128)(2,1)} async-done(((bf16[4,128,768]{2,1,0:T(8,128)(2,1)}), bf16[4,128,768]{2,1,0:T(8,128)(2,1)}, u32[]{:S(2)}, u32[]{:S(2)}) %all-to-all-start.6) | async-done | bytes 786464 | tf_op jit(solution)/shard_map/all_to_all | solution.py:793
  730.4 25.6 %place_pieces.8 = bf16[4,128,768]{2,1,0:T(8,128)(2,1)} custom-call(s32[4]{0:T(128)} %pad_add_fusion.spots_ref, bf16[128,768]{1,0:T(8,128)(2,1)} %reduce_sum.139.refs_0_, bf16[128,768]{1,0:T(8,128)(2,1)} %collective-permute-done.20.refs_1_, bf16[128,768]{1,0:T(8,128)(2,1)} %collective-permute-done.21.refs_2_, bf16[128,768]{1,0:T(8,128)(2,1)} %collective-permute-done.22.refs_3_), custom_call_target="tpu_custom_call" | custom-call | tf_op jit(solution)/shard_map/place_pieces/pallas_call | solution.py:484
  (371 shorter events, 191.7 us)
Async XLA Ops:
  9.8 51.0 %collective-permute-start = (bf16[256,768]{1,0:T(8,128)(2,1)S(1)}, bf16[256,768]{1,0:T(8,128)(2,1)}, u32[]{:S(2)}, u32[]{:S(2)}) collective-permute-start(bf16[256,768]{1,0:T(8,128)(2,1)S(1)} %dynamic-slice_bitcast_fusion.1.refs_0_), channel_id=1, source_target_pairs={{0,2},{2,0},{4,6},{6,4},{1,3},{3,1},{5,7},{7,5},{8,10},{10,8},{12,... | collective-permute-start | bytes 1179656 | tf_op jit(solution)/shard_map/ppermute | solution.py:497
  11.4 49.5 %collective-permute-start.1 = (bf16[256,768]{1,0:T(8,128)(2,1)S(1)}, bf16[256,768]{1,0:T(8,128)(2,1)}, u32[]{:S(2)}, u32[]{:S(2)}) collective-permute-start(bf16[256,768]{1,0:T(8,128)(2,1)S(1)} %dynamic-slice_bitcast_fusion.1.refs_0_), channel_id=1, source_target_pairs={{0,4},{2,6},{4,0},{6,2},{1,5},{3,7},{5,1},{7,3},{8,12},{10,14},{12... | collective-permute-start | bytes 1179656 | tf_op jit(solution)/shard_map/ppermute | solution.py:497
  12.5 16.4 %collective-permute-start.5 = (bf16[128,768]{1,0:T(8,128)(2,1)S(1)}, bf16[128,768]{1,0:T(8,128)(2,1)S(1)}, u32[]{:S(2)}, u32[]{:S(2)}) collective-permute-start(bf16[128,768]{1,0:T(8,128)(2,1)S(1)} %dynamic-slice_select_fusion.refs_0_), channel_id=1, source_target_pairs={{0,16},{8,24},{16,0},{24,8},{1,17},{9,25},{17,1},{25,9},{2,18},{10... | collective-permute-start | bytes 589832 | tf_op jit(solution)/shard_map/ppermute | solution.py:497
  15.1 17.7 %collective-permute-start.6 = (bf16[128,768]{1,0:T(8,128)(2,1)S(1)}, bf16[128,768]{1,0:T(8,128)(2,1)}, u32[]{:S(2)}, u32[]{:S(2)}) collective-permute-start(bf16[128,768]{1,0:T(8,128)(2,1)S(1)} %dynamic-slice_select_fusion.refs_0_), channel_id=1, source_target_pairs={{0,24},{8,16},{16,8},{24,0},{1,25},{9,17},{17,9},{25,1},{2,26},{10... | collective-permute-start | bytes 589832 | tf_op jit(solution)/shard_map/ppermute | solution.py:497
  20.2 40.6 %collective-permute-start.2 = (bf16[256,768]{1,0:T(8,128)(2,1)S(1)}, bf16[256,768]{1,0:T(8,128)(2,1)S(1)}, u32[]{:S(2)}, u32[]{:S(2)}) collective-permute-start(bf16[256,768]{1,0:T(8,128)(2,1)S(1)} %dynamic-slice_bitcast_fusion.1.refs_0_), channel_id=1, source_target_pairs={{0,6},{2,4},{4,2},{6,0},{1,7},{3,5},{5,3},{7,1},{8,14},{10,12},{12... | collective-permute-start | bytes 1179656 | tf_op jit(solution)/shard_map/ppermute | solution.py:497
  58.4 52.7 %collective-permute-start.7 = (bf16[4,128,768]{2,1,0:T(8,128)(2,1)}, bf16[4,128,768]{2,1,0:T(8,128)(2,1)S(1)}, u32[]{:S(2)}, u32[]{:S(2)}) collective-permute-start(bf16[4,128,768]{2,1,0:T(8,128)(2,1)} %place_pieces.6), channel_id=1, source_target_pairs={{0,1},{1,0},{2,3},{3,2},{4,5},{5,4},{6,7},{7,6},{8,9},{9,8},{10,11... | collective-permute-start | bytes 2359304 | tf_op jit(solution)/shard_map/ppermute | solution.py:467
  113.8 39.0 %collective-permute-start.8 = (bf16[48,3456]{1,0:T(8,128)(2,1)}, bf16[48,3456]{1,0:T(8,128)(2,1)}, u32[]{:S(2)}, u32[]{:S(2)}) collective-permute-start(bf16[48,3456]{1,0:T(8,128)(2,1)} %get-tuple-element.119), channel_id=1, source_target_pairs={{0,8},{8,0},{16,24},{24,16},{1,9},{9,1},{17,25},{25,17},{2,10},{10... | collective-permute-start | bytes 995336 | tf_op jit(solution)/shard_map/ppermute | solution.py:497
  113.8 39.0 %collective-permute-start.9 = (bf16[48,3456]{1,0:T(8,128)(2,1)}, bf16[48,3456]{1,0:T(8,128)(2,1)}, u32[]{:S(2)}, u32[]{:S(2)}) collective-permute-start(bf16[48,3456]{1,0:T(8,128)(2,1)} %get-tuple-element.119), channel_id=1, source_target_pairs={{0,16},{8,24},{16,0},{24,8},{1,17},{9,25},{17,1},{25,9},{2,18},{10... | collective-permute-start | bytes 995336 | tf_op jit(solution)/shard_map/ppermute | solution.py:497
  116.8 36.0 %collective-permute-start.10 = (bf16[48,3456]{1,0:T(8,128)(2,1)}, bf16[48,3456]{1,0:T(8,128)(2,1)}, u32[]{:S(2)}, u32[]{:S(2)}) collective-permute-start(bf16[48,3456]{1,0:T(8,128)(2,1)} %get-tuple-element.119), channel_id=1, source_target_pairs={{0,24},{8,16},{16,8},{24,0},{1,25},{9,17},{17,9},{25,1},{2,26},{10... | collective-permute-start | bytes 995336 | tf_op jit(solution)/shard_map/ppermute | solution.py:497
  155.8 51.8 %collective-permute-start.11 = (bf16[3,48,3456]{2,1,0:T(8,128)(2,1)}, bf16[3,48,3456]{2,1,0:T(8,128)(2,1)}, u32[]{:S(2)}, u32[]{:S(2)}) collective-permute-start(bf16[3,48,3456]{2,1,0:T(8,128)(2,1)} %pad_maximum_fusion.4), channel_id=1, source_target_pairs={{0,2},{2,0},{4,6},{6,4},{1,3},{3,1},{5,7},{7,5},{8,10},{10,8},{12,... | collective-permute-start | bytes 2985992 | tf_op jit(solution)/shard_map/ppermute | solution.py:497
  157.1 50.5 %collective-permute-start.12 = (bf16[3,48,3456]{2,1,0:T(8,128)(2,1)}, bf16[3,48,3456]{2,1,0:T(8,128)(2,1)}, u32[]{:S(2)}, u32[]{:S(2)}) collective-permute-start(bf16[3,48,3456]{2,1,0:T(8,128)(2,1)} %pad_maximum_fusion.4), channel_id=1, source_target_pairs={{0,4},{2,6},{4,0},{6,2},{1,5},{3,7},{5,1},{7,3},{8,12},{10,14},{12... | collective-permute-start | bytes 2985992 | tf_op jit(solution)/shard_map/ppermute | solution.py:497
  157.9 49.7 %collective-permute-start.13 = (bf16[3,48,3456]{2,1,0:T(8,128)(2,1)}, bf16[3,48,3456]{2,1,0:T(8,128)(2,1)}, u32[]{:S(2)}, u32[]{:S(2)}) collective-permute-start(bf16[3,48,3456]{2,1,0:T(8,128)(2,1)} %pad_maximum_fusion.4), channel_id=1, source_target_pairs={{0,6},{2,4},{4,2},{6,0},{1,7},{3,5},{5,3},{7,1},{8,14},{10,12},{12... | collective-permute-start | bytes 2985992 | tf_op jit(solution)/shard_map/ppermute | solution.py:497
  384.1 16.4 %collective-permute-start.15 = (bf16[768,3072]{1,0:T(8,128)(2,1)}, bf16[768,3072]{1,0:T(8,128)(2,1)}, u32[]{:S(2)}, u32[]{:S(2)}) collective-permute-start(bf16[768,3072]{1,0:T(8,128)(2,1)} %slice.244), channel_id=1, source_target_pairs={{0,1},{1,0},{2,3},{3,2},{4,5},{5,4},{6,7},{7,6},{8,9},{9,8},{10,11... | collective-permute-start | bytes 14155784 | tf_op jit(solution)/shard_map/ppermute | solution.py:467
  429.0 17.7 %all-to-all-start.1 = ((bf16[4,256,192]{1,2,0:T(8,128)(2,1)}), bf16[4,256,192]{1,2,0:T(8,128)(2,1)}, u32[]{:S(2)}, u32[]{:S(2)}) async-start(bf16[4,256,192]{1,2,0:T(8,128)(2,1)} %bitcast.208), calls=%async_computation.1 | async-start | bytes 786432 | tf_op jit(solution)/shard_map/all_to_all | solution.py:726
  446.7 41.3 %all-to-all-start.2 = ((bf16[4,4,48,2048]{3,2,1,0:T(8,128)(2,1)}), bf16[4,4,48,2048]{3,2,1,0:T(8,128)(2,1)}, u32[]{:S(2)}, u32[]{:S(2)}) async-start(bf16[4,4,48,2048]{3,2,1,0:T(8,128)(2,1)} %slice.248), calls=%async_computation.2 | async-start | bytes 6291456 | tf_op jit(solution)/shard_map/all_to_all | solution.py:719
  487.9 55.5 %all-to-all-start.4 = ((bf16[4,4,48,1408]{3,2,1,0:T(8,128)(2,1)}), bf16[4,4,48,1408]{3,2,1,0:T(8,128)(2,1)}, u32[]{:S(2)}, u32[]{:S(2)}) async-start(bf16[4,4,48,1408]{3,2,1,0:T(8,128)(2,1)} %slice.249), calls=%async_computation.4 | async-start | bytes 4325376 | tf_op jit(solution)/shard_map/all_to_all | solution.py:720
  543.4 53.6 %all-to-all-start.3 = ((bf16[4,48,2048]{2,1,0:T(8,128)(2,1)}), bf16[4,48,2048]{2,1,0:T(8,128)(2,1)}, u32[]{:S(2)}, u32[]{:S(2)}) async-start(bf16[4,48,2048]{2,1,0:T(8,128)(2,1)} %reduce_sum.135), calls=%async_computation.3 | async-start | bytes 1572864 | tf_op jit(solution)/shard_map/all_to_all | solution.py:741
  599.9 15.9 %all-to-all-start.7 = ((bf16[4,48,1408]{2,1,0:T(8,128)(2,1)}), bf16[4,48,1408]{2,1,0:T(8,128)(2,1)}, u32[]{:S(2)}, u32[]{:S(2)}) async-start(bf16[4,48,1408]{2,1,0:T(8,128)(2,1)} %reduce_sum.142), calls=%async_computation.7 | async-start | bytes 1081344 | tf_op jit(solution)/shard_map/all_to_all | solution.py:759
  612.1 18.1 %collective-permute-start.19 = (bf16[4,128,768]{2,1,0:T(8,128)(2,1)}, bf16[4,128,768]{2,1,0:T(8,128)(2,1)}, u32[]{:S(2)}, u32[]{:S(2)}) collective-permute-start(bf16[4,128,768]{2,1,0:T(8,128)(2,1)} %fusion.49), channel_id=1, source_target_pairs={{0,1},{1,0},{2,3},{3,2},{4,5},{5,4},{6,7},{7,6},{8,9},{9,8},{10,11... | collective-permute-start | bytes 2359304 | tf_op jit(solution)/shard_map/ppermute | solution.py:467
  615.9 78.9 %all-to-all-start.5 = ((bf16[4,256,768]{2,1,0:T(8,128)(2,1)}), bf16[4,256,768]{2,1,0:T(8,128)(2,1)}, u32[]{:S(2)}, u32[]{:S(2)}) async-start(bf16[4,256,768]{2,1,0:T(8,128)(2,1)} %bitcast.197), calls=%async_computation.5 | async-start | bytes 3145728 | tf_op jit(solution)/shard_map/all_to_all | solution.py:644
  625.6 22.4 %collective-permute-start.24 = (bf16[48,3456]{1,0:T(8,128)(2,1)S(1)}, bf16[48,3456]{1,0:T(8,128)(2,1)S(1)}, u32[]{:S(2)}, u32[]{:S(2)}) collective-permute-start(bf16[48,3456]{1,0:T(8,128)(2,1)S(1)} %pad_maximum_fusion.9.refs_0_), channel_id=1, source_target_pairs={{0,2},{2,0},{4,6},{6,4},{1,3},{3,1},{5,7},{7,5},{8,10},{10,8},{12,... | collective-permute-start | bytes 995336 | tf_op jit(solution)/shard_map/ppermute | solution.py:497
  627.1 20.9 %collective-permute-start.25 = (bf16[48,3456]{1,0:T(8,128)(2,1)S(1)}, bf16[48,3456]{1,0:T(8,128)(2,1)S(1)}, u32[]{:S(2)}, u32[]{:S(2)}) collective-permute-start(bf16[48,3456]{1,0:T(8,128)(2,1)S(1)} %pad_maximum_fusion.9.refs_0_), channel_id=1, source_target_pairs={{0,4},{2,6},{4,0},{6,2},{1,5},{3,7},{5,1},{7,3},{8,12},{10,14},{12... | collective-permute-start | bytes 995336 | tf_op jit(solution)/shard_map/ppermute | solution.py:497
  627.7 25.1 %collective-permute-start.26 = (bf16[48,3456]{1,0:T(8,128)(2,1)S(1)}, bf16[48,3456]{1,0:T(8,128)(2,1)}, u32[]{:S(2)}, u32[]{:S(2)}) collective-permute-start(bf16[48,3456]{1,0:T(8,128)(2,1)S(1)} %pad_maximum_fusion.9.refs_0_), channel_id=1, source_target_pairs={{0,6},{2,4},{4,2},{6,0},{1,7},{3,5},{5,3},{7,1},{8,14},{10,12},{12... | collective-permute-start | bytes 995336 | tf_op jit(solution)/shard_map/ppermute | solution.py:497
  694.8 23.4 %all-to-all-start.6 = ((bf16[4,128,768]{2,1,0:T(8,128)(2,1)}), bf16[4,128,768]{2,1,0:T(8,128)(2,1)}, u32[]{:S(2)}, u32[]{:S(2)}) async-start(bf16[4,128,768]{2,1,0:T(8,128)(2,1)} %add_convert_fusion.1), calls=%async_computation.6 | async-start | bytes 1572864 | tf_op jit(solution)/shard_map/all_to_all | solution.py:793
  (73 other events, 826.0 us)
